TPU v7x, 32 devices: a whole 2x2x4 slice. The times are simulated.
32 devices in a mesh: dp: 16 (over z, y, x), shard: 2 (over core).
Axes of the slice: x: 2, y: 2, z: 4, core: 2. Of those that a mesh axis runs over, the one named last changes fastest.
Arguments:
- features: bfloat16 [24576, 1024], P('dp'), may hold values from -6 to 6
- condition: bfloat16 [1536, 1152], P('dp'), may hold values from -6 to 6
- task_ids: int32 [1536], P('dp'), may hold values from 0 to 49, never falling along the last dimension, each value on 1 to 61 neighbouring positions
- conv_first: bfloat16 [5, 1024, 1024], P(None, 'dp', 'shard'), may hold values from -0.078125 to 0.078125
- conv_second: bfloat16 [5, 1024, 1024], P(None, 'dp', 'shard'), may hold values from -0.078125 to 0.078125
- film_weight: bfloat16 [1152, 2048], P('dp', 'shard'), may hold values from -0.1875 to 0.1875
- norm_gain_first: bfloat16 [1024], P(('dp', 'shard')), may hold values from 0.099609375 to 1.8984375
- norm_shift_first: bfloat16 [1024], P(('dp', 'shard')), may hold values from -3 to 3
- norm_gain_second: bfloat16 [1024], P(('dp', 'shard')), may hold values from 0.099609375 to 1.8984375
- norm_shift_second: bfloat16 [1024], P(('dp', 'shard')), may hold values from -3 to 3
- film_bias: bfloat16 [2048], P(('dp', 'shard')), may hold values from -3 to 3
- task_table: bfloat16 [50, 1152], replicated, may hold values from -3 to 3
- out_grad: bfloat16 [24576, 1024], P('dp'), may hold values from -6 to 6
- grad_mask: int32 [24576], P('dp'), may hold values 0 or 1
Outputs:
- block_out: bfloat16 [24576, 1024], P('dp')
- grad_features: bfloat16 [24576, 1024], P('dp')
- grad_conv_first: float32 [5, 1024, 1024], P(None, 'dp', 'shard')
- grad_conv_second: float32 [5, 1024, 1024], P(None, 'dp', 'shard')
- grad_film_weight: float32 [1152, 2048], P('dp', 'shard')
- grad_gain_first: float32 [1024], P(('dp', 'shard'))
- grad_shift_first: float32 [1024], P(('dp', 'shard'))
- grad_gain_second: float32 [1024], P(('dp', 'shard'))
- grad_shift_second: float32 [1024], P(('dp', 'shard'))
- grad_film_bias: float32 [2048], P(('dp', 'shard'))
- grad_task_table: float32 [50, 1152], replicated
Inputs may be any that keep to these rules, and one draw needn't show every extreme that they name: `task_ids`: task numbers never fall along the samples; every task has one or more samples.
All inputs are finite; a program needn't handle non-finite values. No bound on the sum of `grad_mask` on one device may be relied on, other than what follows from the above.
Results may differ from a plain program's by a relative error of at most 0.0064.
Values may be sent and summed in bfloat16 or wider, within the bound.
No kernel may reach another device: no remote copies, remote signals or barrier semaphores. Data moves between devices by JAX's collectives and lax.ppermute only.
A program may use at most 256 MiB of HBM per device.

v0:
```python
import jax
import jax.numpy as jnp
from jax import lax
from jax.sharding import PartitionSpec as P

KERNEL = 5
GROUPS = 8
HORIZON = 16


epsilon = 1e-05


def mish_act(values):
    return values * jnp.tanh(jax.nn.softplus(values))


def mish_slope(values):
    tangent = jnp.tanh(jax.nn.softplus(values))
    return tangent + values * (1.0 - tangent * tangent) * jax.nn.sigmoid(values)


def shifted(values, offset):
    horizon = values.shape[1]
    half_kernel = KERNEL // 2
    padded = jnp.pad(values, ((0, 0), (half_kernel, half_kernel), (0, 0)))
    return lax.slice_in_dim(padded, half_kernel + offset, half_kernel + offset + horizon, axis=1)


def unfold(values, sign):
    half_kernel = KERNEL // 2
    stacked = jnp.stack(
        [shifted(values, sign * (offset - half_kernel)) for offset in range(KERNEL)], axis=2
    )
    return stacked.reshape(values.shape[0] * values.shape[1], KERNEL * values.shape[2])


def conv_apply(values, weight):
    samples, horizon, channel_count = values.shape
    result = jnp.dot(
        unfold(values, 1),
        weight.reshape(KERNEL * channel_count, weight.shape[2]),
        preferred_element_type=jnp.float32,
    )
    return result.reshape(samples, horizon, weight.shape[2])


def conv_transpose(grads, weight):
    samples, horizon, channel_count = grads.shape
    columns = unfold(grads, -1).reshape(samples * horizon, KERNEL, channel_count)
    result = jnp.einsum("fko,kio->fi", columns, weight, preferred_element_type=jnp.float32)
    return result.reshape(samples, horizon, weight.shape[1])


def conv_weight_grad(values, grads, column, quarter):
    samples, horizon, channel_count = values.shape
    part = lax.dynamic_slice_in_dim(
        grads.reshape(samples * horizon, grads.shape[2]), column * quarter, quarter, 1
    )
    result = jnp.einsum("fa,fb->ab", unfold(values, 1), part, preferred_element_type=jnp.float32)
    return result.reshape(KERNEL, channel_count, quarter)


def normalize(activations):
    samples, horizon, channel_count = activations.shape
    grouped = activations.reshape(samples, horizon, GROUPS, channel_count // GROUPS)
    centre = grouped - jnp.mean(grouped, axis=(1, 3), keepdims=True)
    spread = lax.rsqrt(jnp.mean(centre * centre, axis=(1, 3), keepdims=True) + epsilon)
    return ((centre * spread).reshape(activations.shape), spread)


def normalize_back(grad_hat, unit, spread):
    samples, horizon, channel_count = grad_hat.shape
    grouped_grad = grad_hat.reshape(samples, horizon, GROUPS, channel_count // GROUPS)
    grouped_unit = unit.reshape(samples, horizon, GROUPS, channel_count // GROUPS)
    mean_grad = jnp.mean(grouped_grad, axis=(1, 3), keepdims=True)
    mean_cross = jnp.mean(grouped_grad * grouped_unit, axis=(1, 3), keepdims=True)
    return (spread * (grouped_grad - mean_grad - grouped_unit * mean_cross)).reshape(grad_hat.shape)


def fetch_weights(conv_first, conv_second, film_weight):
    rows_a, rows_b, rows_film = (
        lax.all_gather(conv_first, "dp", axis=1, tiled=True),
        lax.all_gather(conv_second, "dp", axis=1, tiled=True),
        lax.all_gather(film_weight, "dp", axis=0, tiled=True),
    )
    return (
        lax.all_gather(rows_a, "shard", axis=2, tiled=True),
        lax.all_gather(rows_b, "shard", axis=2, tiled=True),
        lax.all_gather(rows_film, "shard", axis=1, tiled=True),
    )


def fetch_vectors(gain_first, shift_first, gain_second, shift_second, film_bias):
    return (
        lax.all_gather(gain_first, ("dp", "shard"), axis=0, tiled=True),
        lax.all_gather(shift_first, ("dp", "shard"), axis=0, tiled=True),
        lax.all_gather(gain_second, ("dp", "shard"), axis=0, tiled=True),
        lax.all_gather(shift_second, ("dp", "shard"), axis=0, tiled=True),
        lax.all_gather(film_bias, ("dp", "shard"), axis=0, tiled=True),
    )


def forward(features, condition, task_ids, task_table, weights, vectors):
    conv_a, conv_b, film_w = weights
    gain_a, shift_a, gain_b, shift_b, film_b = [member.astype(jnp.float32) for member in vectors]
    samples = condition.shape[0]
    channel_count = conv_a.shape[2]
    inputs = features.reshape(samples, HORIZON, channel_count)
    unit_a, spread_a = normalize(conv_apply(inputs, conv_a))
    normed_a = unit_a * gain_a + shift_a
    mixed_a = mish_act(normed_a)
    onehot = (task_ids[:, None] == jnp.arange(task_table.shape[0])[None, :]).astype(jnp.float32)
    cond_in = condition.astype(jnp.float32) + jnp.dot(
        onehot, task_table.astype(jnp.float32), precision=lax.Precision.HIGHEST
    )
    embedded = mish_act(cond_in).astype(jnp.bfloat16)
    film_out = jnp.dot(embedded, film_w, preferred_element_type=jnp.float32) + film_b
    film_scale = film_out[:, None, :channel_count]
    lifted = (film_scale * mixed_a + film_out[:, None, channel_count:]).astype(jnp.bfloat16)
    unit_b, spread_b = normalize(conv_apply(lifted, conv_b))
    normed_b = unit_b * gain_b + shift_b
    output = inputs.astype(jnp.float32) + mish_act(normed_b)
    saved_state = (
        inputs,
        unit_a,
        spread_a,
        normed_a,
        mixed_a,
        onehot,
        cond_in,
        embedded,
        film_scale,
        lifted,
        unit_b,
        spread_b,
        normed_b,
    )
    return (output.reshape(samples * HORIZON, channel_count).astype(jnp.bfloat16), saved_state)


def own_slice(vector, dp_count, shard_count, column):
    return lax.dynamic_index_in_dim(
        vector.reshape(dp_count, shard_count, -1), column, axis=1, keepdims=False
    )


def backward(saved_state, weights, vectors, out_grad, grad_mask):
    (
        inputs,
        unit_a,
        spread_a,
        normed_a,
        mixed_a,
        onehot,
        cond_in,
        embedded,
        film_scale,
        lifted,
        unit_b,
        spread_b,
        normed_b,
    ) = saved_state
    conv_a, conv_b, film_w = weights
    gain_a = vectors[0].astype(jnp.float32)
    gain_b = vectors[2].astype(jnp.float32)
    samples, horizon, channel_count = inputs.shape
    shard_count = lax.axis_size("shard")
    dp_count = lax.axis_size("dp")
    column = lax.axis_index("shard")
    quarter = channel_count // shard_count
    upstream = (out_grad.astype(jnp.float32) * grad_mask.astype(jnp.float32)[:, None]).reshape(
        samples, horizon, channel_count
    )
    grad_normed_b = upstream * mish_slope(normed_b)
    grad_gain_b = jnp.sum(grad_normed_b * unit_b, axis=(0, 1))
    grad_shift_b = jnp.sum(grad_normed_b, axis=(0, 1))
    grad_second = normalize_back(grad_normed_b * gain_b, unit_b, spread_b).astype(jnp.bfloat16)
    grad_conv_b = conv_weight_grad(lifted, grad_second, column, quarter)
    grad_lifted = conv_transpose(grad_second, conv_b)
    grad_mixed_a = grad_lifted * film_scale
    grad_film = jnp.concatenate(
        [jnp.sum(grad_lifted * mixed_a, axis=1), jnp.sum(grad_lifted, axis=1)], axis=1
    )
    grad_film_bias = jnp.sum(grad_film, axis=0)
    grad_film_low = grad_film.astype(jnp.bfloat16)
    film_cols = 2 * channel_count // shard_count
    film_part = lax.dynamic_slice_in_dim(grad_film_low, column * film_cols, film_cols, 1)
    grad_film_w = jnp.einsum("sa,sb->ab", embedded, film_part, preferred_element_type=jnp.float32)
    grad_embedded = jnp.einsum(
        "sb,ab->sa", grad_film_low, film_w, preferred_element_type=jnp.float32
    )
    grad_cond = grad_embedded * mish_slope(cond_in)
    grad_table = jnp.dot(onehot.T, grad_cond, precision=lax.Precision.HIGHEST)
    grad_normed_a = grad_mixed_a * mish_slope(normed_a)
    grad_gain_a = jnp.sum(grad_normed_a * unit_a, axis=(0, 1))
    grad_shift_a = jnp.sum(grad_normed_a, axis=(0, 1))
    grad_first = normalize_back(grad_normed_a * gain_a, unit_a, spread_a).astype(jnp.bfloat16)
    grad_conv_a = conv_weight_grad(inputs, grad_first, column, quarter)
    grad_inputs = upstream + conv_transpose(grad_first, conv_a)
    summed = (
        lax.psum_scatter(grad_conv_a, "dp", scatter_dimension=1, tiled=True),
        lax.psum_scatter(grad_conv_b, "dp", scatter_dimension=1, tiled=True),
        lax.psum_scatter(grad_film_w, "dp", scatter_dimension=0, tiled=True),
        lax.psum_scatter(
            own_slice(grad_gain_a, dp_count, shard_count, column),
            "dp",
            scatter_dimension=0,
            tiled=True,
        ),
        lax.psum_scatter(
            own_slice(grad_shift_a, dp_count, shard_count, column),
            "dp",
            scatter_dimension=0,
            tiled=True,
        ),
        lax.psum_scatter(
            own_slice(grad_gain_b, dp_count, shard_count, column),
            "dp",
            scatter_dimension=0,
            tiled=True,
        ),
        lax.psum_scatter(
            own_slice(grad_shift_b, dp_count, shard_count, column),
            "dp",
            scatter_dimension=0,
            tiled=True,
        ),
        lax.psum_scatter(
            own_slice(grad_film_bias, dp_count, shard_count, column),
            "dp",
            scatter_dimension=0,
            tiled=True,
        ),
    )
    table_total = lax.psum(grad_table, "dp")
    grad_features = grad_inputs.reshape(samples * horizon, channel_count).astype(jnp.bfloat16)
    return (
        grad_features,
        summed[0],
        summed[1],
        summed[2],
        summed[3].reshape(-1),
        summed[4].reshape(-1),
        summed[5].reshape(-1),
        summed[6].reshape(-1),
        summed[7].reshape(-1),
        table_total,
    )


def local(
    features,
    condition,
    task_ids,
    conv_first,
    conv_second,
    film_weight,
    norm_gain_first,
    norm_shift_first,
    norm_gain_second,
    norm_shift_second,
    film_bias,
    task_table,
    out_grad,
    grad_mask,
):
    weights = fetch_weights(conv_first, conv_second, film_weight)
    vectors = fetch_vectors(
        norm_gain_first, norm_shift_first, norm_gain_second, norm_shift_second, film_bias
    )
    block_out, saved_state = forward(features, condition, task_ids, task_table, weights, vectors)
    weights = fetch_weights(conv_first, conv_second, film_weight)
    vectors = fetch_vectors(
        norm_gain_first, norm_shift_first, norm_gain_second, norm_shift_second, film_bias
    )
    unused_out, saved_state = forward(features, condition, task_ids, task_table, weights, vectors)
    grads = backward(saved_state, weights, vectors, out_grad, grad_mask)
    return (
        block_out,
        grads[0],
        grads[1],
        grads[2],
        grads[3],
        grads[4],
        grads[5],
        grads[6],
        grads[7],
        grads[8],
        grads[9],
    )


def solution(mesh):
    return jax.shard_map(
        local,
        mesh=mesh,
        in_specs=(
            P("dp", None),
            P("dp", None),
            P("dp"),
            P(None, "dp", "shard"),
            P(None, "dp", "shard"),
            P("dp", "shard"),
            P(("dp", "shard")),
            P(("dp", "shard")),
            P(("dp", "shard")),
            P(("dp", "shard")),
            P(("dp", "shard")),
            P(),
            P("dp", None),
            P("dp"),
        ),
        out_specs=(
            P("dp", None),
            P("dp", None),
            P(None, "dp", "shard"),
            P(None, "dp", "shard"),
            P("dp", "shard"),
            P(("dp", "shard")),
            P(("dp", "shard")),
            P(("dp", "shard")),
            P(("dp", "shard")),
            P(("dp", "shard")),
            P(),
        ),
        check_vma=False,
    )
```

profile of v0, /device:TPU:10, one launch (start us, length us, event | category | flops | bytes accessed | tf_op | source)
XLA Modules:
  0.0 1246.5 jit_solution(10214625582569122753)
XLA Ops:
  9.5 65.2 %all-gather.7.cloned.1.call-done = bf16[1152,1024]{1,0:T(8,128)(2,1)} async-done(((bf16[72,1024]{1,0:T(8,128)(2,1)}), bf16[1152,1024]{1,0:T(8,128)(2,1)}) %all-gather.7.cloned.1.call-update) | async-done | bytes 2359312 | tf_op jit(solution)/shard_map/all_gather | solution.py:85
  74.8 85.7 %all-gather.11.cloned.1.call-done = bf16[5,1024,512]{2,1,0:T(8,128)(2,1)} async-done(((bf16[5,64,512]{2,1,0:T(8,128)(2,1)}), bf16[5,1024,512]{2,1,0:T(8,128)(2,1)}) %all-gather.11.cloned.1.call-update) | async-done | bytes 5242896 | tf_op jit(solution)/shard_map/all_gather | solution.py:83
  161.8 39.8 %all-reduce.15 = (bf16[2048]{0:T(1024)(128)(2,1)S(1)}, bf16[1024]{0:T(1024)(128)(2,1)S(1)}, bf16[1024]{0:T(1024)(128)(2,1)S(1)}, bf16[1024]{0:T(1024)(128)(2,1)S(1)}, bf16[1024]{0:T(1024)(128)(2,1)S(1)}) all-reduce(bf16[2048]{0:T(1024)(128)(2,1)S(1)} %dynamic-update-slice, ...), channel_id=1, replica_groups=mesh['dp'=16,'shard'=2] {'dp','shard'}, use_global_device_ids=true, to_apply=%add.4 | all-reduce | flops 6144 | bytes 24576
  221.5 26.6 %copy.137 = bf16[96,16,5,1024]{0,3,2,1:T(8,128)(2,1)} copy(bf16[96,16,5,1024]{3,1,0,2:T(8,128)(2,1)} %fusion.28) | data formatting | bytes 31457280 | tf_op jit(solution)/shard_map/stack | solution.py:32
  249.2 13.5 %all-gather.9.cloned.1.call-done = bf16[1152,2048]{1,0:T(8,128)(2,1)} async-done(((bf16[1152,1024]{1,0:T(8,128)(2,1)}), bf16[1152,2048]{1,0:T(8,128)(2,1)}) %all-gather.9.cloned.1.call-update) | async-done | bytes 4718608 | tf_op jit(solution)/shard_map/all_gather | solution.py:90
  266.2 22.0 %all-gather.13.cloned.1.call-done = bf16[5,1024,1024]{2,1,0:T(8,128)(2,1)} async-done(((bf16[5,1024,512]{2,1,0:T(8,128)(2,1)}), bf16[5,1024,1024]{2,1,0:T(8,128)(2,1)}) %all-gather.13.cloned.1.call-update) | async-done | bytes 10485776 | tf_op jit(solution)/shard_map/all_gather | solution.py:88
  288.2 14.3 %copy.138 = bf16[5120,1024]{0,1:T(8,128)(2,1)} copy(bf16[5120,1024]{1,0:T(8,128)(2,1)} %bitcast.252) | data formatting | bytes 20971520 | tf_op jit(solution)/shard_map/reshape | solution.py:42
  302.5 29.2 %fusion.88 = (f32[96,8]{0,1:T(8,128)S(1)}, f32[96,16,8,128]{3,0,2,1:T(8,128)S(1)}) fusion(bf16[96,16,5120,1]{0,2,3,1:T(8,128)(2,1)} %bitcast.246, bf16[8,128,5120,1]{2,1,0,3:T(8,128)(2,1)} %bitcast.255), kind=kOutput, calls=%fused_computation.159 | convolution fusion | flops 16107699200 | bytes 32508928 | tf_op jit(solution)/shard_map/dot_general | solution.py:40
  340.6 7.1 reshape.298
  347.7 7.1 reshape.299
  354.9 14.0 %copy.143 = bf16[5120,1024]{0,1:T(8,128)(2,1)} copy(bf16[5120,1024]{1,0:T(8,128)(2,1)} %bitcast.253) | data formatting | bytes 20971520 | tf_op jit(solution)/shard_map/reshape | solution.py:42
  368.9 6.6 add_convert_fusion
  394.1 26.6 %copy.142 = bf16[96,16,5,1024]{0,3,2,1:T(8,128)(2,1)} copy(bf16[96,16,5,1024]{3,1,0,2:T(8,128)(2,1)} %fusion.36) | data formatting | bytes 31457280 | tf_op jit(solution)/shard_map/stack | solution.py:32
  420.7 30.3 %fusion.89 = (f32[96,8]{0,1:T(8,128)S(1)}, f32[96,16,8,128]{3,0,2,1:T(8,128)}) fusion(bf16[96,16,5120,1]{0,2,3,1:T(8,128)(2,1)} %bitcast.247, bf16[8,128,5120,1]{2,1,0,3:T(8,128)(2,1)} %bitcast.254), kind=kOutput, calls=%fused_computation.160 | convolution fusion | flops 16107699200 | bytes 32508928 | tf_op jit(solution)/shard_map/dot_general | solution.py:40
  455.6 11.5 multiply_reduce_fusion.1
  497.0 31.9 %fusion.82 = (f32[1024]{0:T(1024)S(1)}, f32[1024]{0:T(1024)S(1)}, f32[96,1024]{1,0:T(8,128)S(1)}, f32[96,1024]{1,0:T(8,128)S(1)}, f32[96,16,1024]{2,1,0:T(8,128)}) fusion(f32[96,16,1024]{2,1,0:T(8,128)} %reshape.298, f32[1024]{0:T(1024)S(1)} %convert_element_type.159, f32[1024]{0:T(1024)S(1)} %convert_element_type.158, f32[96,1024]{1,0:T(8,128)S(1)} %copy-done.15, ...), kind=kOutput, calls=%fused_computation.154 | convolution fusion | flops 16145250304 | bytes 39993344 | tf_op jit(solution)/shard_map/fko,kio->fi/dot_general | solution.py:51
  538.1 17.3 %copy.165 = bf16[96,16,5,1024]{3,2,1,0:T(8,128)(2,1)S(1)} copy(bf16[96,16,5,1024]{3,1,0,2:T(8,128)(2,1)} %fusion.36) | data formatting | bytes 31457280 | tf_op jit(solution)/shard_map/stack | solution.py:32
  556.2 15.8 %copy.182 = bf16[192,8,5,1024]{3,1,2,0:T(8,128)(2,1)} copy(bf16[192,8,5,1024]{3,2,1,0:T(8,128)(2,1)S(1)} %bitcast.229) | data formatting | bytes 31457280
  572.0 20.7 %copy.166 = bf16[5120,1536]{1,0:T(8,128)(2,1)} copy(bf16[5120,1536]{0,1:T(8,128)(2,1)} %bitcast.233) | data formatting | bytes 31457280 | tf_op jit(solution)/shard_map/fa,fb->ab/dot_general | solution.py:60
  592.7 14.1 %fusion.55 = f32[5,1024,512]{2,1,0:T(8,128)} fusion(bf16[5,1024,1536]{2,1,0:T(8,128)(2,1)} %bitcast.251, bf16[1536,1024]{1,0:T(8,128)(2,1)S(1)} %bitcast.258, s32[]{:T(128)S(6)} %select_n.52), kind=kOutput, calls=%fused_computation.104 | convolution fusion | flops 8053063680 | bytes 27787268 | tf_op jit(solution)/shard_map/fa,fb->ab/dot_general | solution.py:60
  606.9 22.7 %copy.162 = bf16[96,16,5,1024]{3,2,1,0:T(8,128)(2,1)} copy(bf16[96,16,5,1024]{3,1,0,2:T(8,128)(2,1)} %fusion.28) | data formatting | bytes 31457280 | tf_op jit(solution)/shard_map/stack | solution.py:32
  629.5 23.8 %copy.180 = bf16[192,8,5,1024]{3,1,2,0:T(8,128)(2,1)} copy(bf16[192,8,5,1024]{3,2,1,0:T(8,128)(2,1)} %bitcast.230) | data formatting | bytes 31457280
  653.4 19.0 %copy.163 = bf16[5120,1536]{1,0:T(8,128)(2,1)} copy(bf16[5120,1536]{0,1:T(8,128)(2,1)} %bitcast.234) | data formatting | bytes 31457280 | tf_op jit(solution)/shard_map/fa,fb->ab/dot_general | solution.py:60
  673.0 9.1 copy.145
  682.2 7.0 fusion.84
  694.2 6.3 multiply_reduce_fusion.3
  719.9 11.9 multiply_reduce_fusion
  737.9 68.3 %all-reduce.14 = (f32[16,32]{1,0:T(8,128)S(1)}, f32[16,32]{1,0:T(8,128)S(1)}, f32[16,32]{1,0:T(8,128)S(1)}, f32[16,32]{1,0:T(8,128)S(1)}, f32[16,64]{1,0:T(8,128)S(1)}) all-reduce(f32[16,32]{1,0:T(8,128)S(1)} %bitcast.265, f32[16,32]{1,0:T(8,128)S(1)} %bitcast.264, ...), channel_id=5, replica_groups=mesh['dp'=16,'shard'=2] {'dp'}, use_global_device_ids=true, to_apply=%region_15.16.clone | all-reduce | flops 3072 | bytes 24576
  825.9 10.9 fusion.57
  836.8 23.9 %fusion.13 = bf16[96,16,1024]{2,1,0:T(8,128)(2,1)} fusion(f32[96,16,1024]{2,1,0:T(8,128)} %bitcast.256, bf16[96,16,5,1024]{3,1,2,0:T(8,128)(2,1)} %fusion.52, bf16[5,1024,1024]{2,1,0:T(8,128)(2,1)} %all-gather.13.cloned.1.call-done), kind=kOutput, calls=%fused_computation.19 | convolution fusion | flops 16109273088 | bytes 35651584 | tf_op jit(solution)/shard_map/fko,kio->fi/dot_general | solution.py:51
  860.7 150.7 %reduce-scatter.6.cloned.1.call-done = f32[5,64,512]{2,1,0:T(8,128)} async-done(((f32[5,1024,512]{2,1,0:T(8,128)}), f32[5,64,512]{2,1,0:T(8,128)}) %reduce-scatter.6.cloned.1.call-update) | async-done | bytes 655376 | tf_op jit(solution)/shard_map/reduce_scatter | solution.py:203
  1011.4 226.1 %reduce-scatter.4.cloned.1.call-done = f32[5,64,512]{2,1,0:T(8,128)} async-done(((f32[5,1024,512]{2,1,0:T(8,128)}), f32[5,64,512]{2,1,0:T(8,128)}) %reduce-scatter.4.cloned.1.call-update) | async-done | bytes 655376 | tf_op jit(solution)/shard_map/reduce_scatter | solution.py:202
  (216 shorter events, 151.9 us)
Async XLA Ops:
  7.2 241.6 %copy-start = (bf16[50,1152]{1,0:T(8,128)(2,1)S(1)}, bf16[50,1152]{1,0:T(8,128)(2,1)}, u32[]{:S(2)}) copy-start(bf16[50,1152]{1,0:T(8,128)(2,1)} %param.25) | copy-start | bytes 345604
  7.2 153.4 %copy-start.34 = (bf16[32]{0:T(256)(128)(2,1)S(1)}, bf16[32]{0:T(256)(128)(2,1)}, u32[]{:S(2)}) copy-start(bf16[32]{0:T(256)(128)(2,1)} %param.23) | copy-start | bytes 196
  7.2 153.7 %copy-start.35 = (bf16[32]{0:T(256)(128)(2,1)S(1)}, bf16[32]{0:T(256)(128)(2,1)}, u32[]{:S(2)}) copy-start(bf16[32]{0:T(256)(128)(2,1)} %param.20) | copy-start | bytes 196
  7.2 153.9 %copy-start.36 = (bf16[32]{0:T(256)(128)(2,1)S(1)}, bf16[32]{0:T(256)(128)(2,1)}, u32[]{:S(2)}) copy-start(bf16[32]{0:T(256)(128)(2,1)} %param.21) | copy-start | bytes 196
  7.2 154.1 %copy-start.37 = (bf16[32]{0:T(256)(128)(2,1)S(1)}, bf16[32]{0:T(256)(128)(2,1)}, u32[]{:S(2)}) copy-start(bf16[32]{0:T(256)(128)(2,1)} %param.22) | copy-start | bytes 196
  7.2 154.4 %copy-start.38 = (bf16[64]{0:T(256)(128)(2,1)S(1)}, bf16[64]{0:T(256)(128)(2,1)}, u32[]{:S(2)}) copy-start(bf16[64]{0:T(256)(128)(2,1)} %param.24) | copy-start | bytes 388
  7.2 194.4 %copy-start.31 = (s32[1536]{0:T(1024)S(1)}, s32[1536]{0:T(1024)}, u32[]{:S(2)}) copy-start(s32[1536]{0:T(1024)} %param.27) | copy-start | bytes 18436
  7.3 195.0 %copy-start.11 = (bf16[1536,1024]{1,0:T(8,128)(2,1)S(1)}, bf16[1536,1024]{1,0:T(8,128)(2,1)}, u32[]{:S(2)}) copy-start(bf16[1536,1024]{1,0:T(8,128)(2,1)} %param.26) | copy-start | bytes 9437188
  7.3 67.5 %all-gather.7.cloned.1.call-start = ((), (), s32[]{:S(2)}) async-start(), calls=%async_computation.3 | async-start | bytes 2506752 | tf_op jit(solution)/shard_map/all_gather | solution.py:85
  8.0 152.5 %all-gather.11.cloned.1.call-start = ((), (), s32[]{:S(2)}) async-start(), calls=%async_computation.5 | async-start | bytes 5570560 | tf_op jit(solution)/shard_map/all_gather | solution.py:83
  8.8 240.3 %all-gather.15.cloned.1.call-start = ((), (), s32[]{:S(2)}) async-start(), calls=%async_computation.7 | async-start | bytes 5570560 | tf_op jit(solution)/shard_map/all_gather | solution.py:84
  9.5 253.2 %all-gather.9.cloned.1.call-start = ((), (), s32[]{:S(2)}) async-start(), calls=%async_computation.4 | async-start | bytes 7077888 | tf_op jit(solution)/shard_map/all_gather | solution.py:90
  74.8 213.4 %all-gather.13.cloned.1.call-start = ((), (), s32[]{:S(2)}) async-start(), calls=%async_computation.6 | async-start | bytes 15728640 | tf_op jit(solution)/shard_map/all_gather | solution.py:88
  160.6 194.3 %all-gather.17.cloned.1.call-start = ((), (), s32[]{:S(2)}) async-start(), calls=%async_computation.8 | async-start | bytes 15728640 | tf_op jit(solution)/shard_map/all_gather | solution.py:89
  221.5 27.3 %copy-start.19 = (bf16[96,1152]{1,0:T(8,128)(2,1)S(1)}, bf16[96,1152]{1,0:T(8,128)(2,1)}, u32[]{:S(2)}) copy-start(bf16[96,1152]{1,0:T(8,128)(2,1)} %param.15) | copy-start | bytes 663556
  221.5 27.3 %copy-start.32 = (s32[96]{0:T(128)S(1)}, s32[96]{0:T(128)}, u32[]{:S(2)}) copy-start(s32[96]{0:T(128)} %param.16) | copy-start | bytes 1156
  249.1 17.1 %copy-start.12 = (f32[96,1152]{1,0:T(8,128)}, f32[96,1152]{1,0:T(8,128)S(1)}, u32[]{:S(2)}) copy-start(f32[96,1152]{1,0:T(8,128)S(1)} %convolution_add_fusion) | copy-start | bytes 1327108
  249.1 611.6 %all-reduce.18.cloned.1.call-start = ((), (), s32[]{:S(2)}) async-start(), calls=%async_computation.12 | async-start | bytes 516096 | tf_op jit(solution)/shard_map/psum | solution.py:236
  266.1 115.2 %copy-start.14 = (f32[96,1024]{1,0:T(8,128)}, f32[96,1024]{1,0:T(8,128)S(1)}, u32[]{:S(2)}) copy-start(f32[96,1024]{1,0:T(8,128)S(1)} %get-tuple-element.36) | copy-start | bytes 1179652
  368.9 12.5 %slice-start.2 = ((s8[6291456]{0:T(1024)(128)(4,1)}), s8[4194304]{0:T(1024)(128)(4,1)S(1)}, s32[]{:S(2)}) async-start(s8[6291456]{0:T(1024)(128)(4,1)} %bitcast.239), calls=%async_computation.15 | async-start | bytes 8388608
  420.7 34.1 %slice-start.4 = ((s8[6291456]{0:T(1024)(128)(4,1)}), s8[4194304]{0:T(1024)(128)(4,1)S(1)}, s32[]{:S(2)}) async-start(s8[6291456]{0:T(1024)(128)(4,1)} %bitcast.242), calls=%async_computation.17 | async-start | bytes 8388608
  420.7 34.1 %slice-start.5 = ((s8[6291456]{0:T(1024)(128)(4,1)}), s8[2097152]{0:T(1024)(128)(4,1)S(1)}, s32[]{:S(2)}) async-start(s8[6291456]{0:T(1024)(128)(4,1)} %bitcast.242), calls=%async_computation.18 | async-start | bytes 4194304
  497.0 32.8 %copy-start.13 = (f32[96,1152]{1,0:T(8,128)S(1)}, f32[96,1152]{1,0:T(8,128)}, u32[]{:S(2)}) copy-start(f32[96,1152]{1,0:T(8,128)} %copy-done.12) | copy-start | bytes 1327108
  534.8 325.9 %reduce-scatter.8.cloned.1.call-start = ((), (), s32[]{:S(2)}) async-start(), calls=%async_computation.11 | async-start | bytes 5013504 | tf_op jit(solution)/shard_map/reduce_scatter | solution.py:204
  538.0 473.5 %reduce-scatter.6.cloned.1.call-start = ((), (), s32[]{:S(2)}) async-start(), calls=%async_computation.10 | async-start | bytes 11141120 | tf_op jit(solution)/shard_map/reduce_scatter | solution.py:203
  538.0 17.3 %copy-start.7 = (bf16[96,16,8,128]{3,2,1,0:T(8,128)(2,1)S(1)}, bf16[96,16,8,128]{3,2,1,0:T(8,128)(2,1)}, u32[]{:S(2)}) copy-start(bf16[96,16,8,128]{3,2,1,0:T(8,128)(2,1)} %copy.147) | copy-start | bytes 9437188
  606.8 630.8 %reduce-scatter.4.cloned.1.call-start = ((), (), s32[]{:S(2)}) async-start(), calls=%async_computation.9 | async-start | bytes 11141120 | tf_op jit(solution)/shard_map/reduce_scatter | solution.py:202
  653.4 19.0 %copy-start.39 = (u32[32]{0:T(128)S(1)}, u32[32]{0:T(128)}, u32[]{:S(2)}) copy-start(u32[32]{0:T(128)} %constant.87) | copy-start | bytes 388
  708.0 11.9 copy-start.28
  731.8 80.0 %copy-start.5 = (bf16[96,16,1024]{2,1,0:T(8,128)(2,1)S(1)}, bf16[96,16,1024]{2,1,0:T(8,128)(2,1)}, u32[]{:S(2)}) copy-start(bf16[96,16,1024]{2,1,0:T(8,128)(2,1)} %convert_element_type.171) | copy-start | bytes 9437188
  811.9 14.0 %slice-start.6 = ((s8[15728640]{0:T(1024)(128)(4,1)}), s8[4194304]{0:T(1024)(128)(4,1)S(1)}, s32[]{:S(2)}) async-start(s8[15728640]{0:T(1024)(128)(4,1)} %bitcast.248), calls=%async_computation.19 | async-start | bytes 8388608
  836.8 402.4 %copy-start.1 = (bf16[50,1152]{1,0:T(8,128)(2,1)S(1)}, bf16[50,1152]{1,0:T(8,128)(2,1)}, u32[]{:S(2)}) copy-start(bf16[50,1152]{1,0:T(8,128)(2,1)} %param.25) | copy-start | bytes 345604
  (28 other events, 164.3 us)
Sparse Core Ops, SparseCore 0:
  10.9 63.7 all-gather.6
  77.5 82.9 all-gather.10
  163.3 84.4 all-gather.14
  249.2 13.4 all-gather.8
  264.1 24.0 all-gather.12
  289.6 24.0 all-gather.16
  535.0 107.0 all-reduce.17
  648.6 136.8 reduce-scatter.7
  788.4 222.9 reduce-scatter.5
  1014.2 223.3 reduce-scatter.3
where the time goes:
time: 1260 us; the launch traced here: 1250 us
  waiting for transfers between devices  565 us (45%)
  local copies, waits for them, and re-layouts  341 us (27%)
  matrix products  152 us (12%)
  blocking collectives  108 us (9%)
  other arithmetic  64 us (5%)
  between operations  15.3 us (1%)
    reduce_scatter x1, waiting for transfers between devices, backward(): lax.psum_scatter(grad_conv_a, 'dp', scatter_dimension=1, tiled=True)  226 us
    reduce_scatter x1, waiting for transfers between devices, backward(): lax.psum_scatter(grad_conv_b, 'dp', scatter_dimension=1, tiled=True)  151 us
    unnamed x2, blocking collectives  108 us
    another operation x8, local copies, waits for them, and re-layouts, unfold(): jnp.stack([shifted(values, sign * (offset - half_kernel)) for offset in r...  106 us
    unnamed x134, local copies, waits for them, and re-layouts  104 us
    all_gather x1, waiting for transfers between devices, fetch_weights(): lax.all_gather(conv_first, 'dp', axis=1, tiled=True)  85.7 us
    all_gather x1, waiting for transfers between devices, fetch_weights(): lax.all_gather(film_weight, 'dp', axis=0, tiled=True)  65.2 us
    dot_general x2, matrix products, conv_apply(): jnp.dot(unfold(values, 1), weight.reshape(KERNEL * channel_count, weight....  59.5 us
  transfers between devices with their start and end apart: 10, of which 6 were waited for; matrix products, arithmetic and copies ran while one was open for 30% of the time, Pallas kernels for 0%

commit v1 on v0

v1 whole, which is shorter than its diff:
```python
import functools

import jax
import jax.numpy as jnp
from jax import lax
from jax.experimental import pallas as pl
from jax.experimental.pallas import tpu as pltpu
from jax.sharding import PartitionSpec as P

KERNEL = 5
HALF = KERNEL // 2
HORIZON = 16
GROUP = 128
EPSILON = 1e-05
BLOCK = 16
VMEM_LIMIT = 48 * 1024 * 1024
f32 = jnp.float32
bf16 = jnp.bfloat16


def mish_parts(v):
    w = jnp.exp(jnp.minimum(v, 20.0))
    n = w * (w + 2.0)
    r = 1.0 / (n + 2.0)
    return w, r, n * r


def mish_act(v):
    return v * mish_parts(v)[2]


def mish_slope(v):
    w, r, t = mish_parts(v)
    return t + v * (4.0 * w * (1.0 + w)) * (r * r)


def digits(count):
    bits = count.bit_length() - 1
    small = bits // 3
    return (1 << (bits - 2 * small), 1 << small, 1 << small)


def coordinates(index, sizes):
    _, ny, nx = sizes
    return (index // (ny * nx), (index // nx) % ny, index % nx)


def flat(position, sizes):
    _, ny, nx = sizes
    return (position[0] * ny + position[1]) * nx + position[2]


def move(value, sizes, axis, by):
    count = sizes[0] * sizes[1] * sizes[2]
    pairs = []
    for source in range(count):
        position = list(coordinates(source, sizes))
        position[axis] = (position[axis] + by) % sizes[axis]
        pairs.append((source, flat(position, sizes)))
    return lax.ppermute(value, "dp", pairs)


def swap(value, by):
    count = lax.axis_size("shard")
    return lax.ppermute(value, "shard", [(i, (i + by) % count) for i in range(count)])


def around(value):
    return [value] + [swap(value, r) for r in range(1, lax.axis_size("shard"))]


def gather_pieces(own, cut, sizes):
    nz, ny, nx = sizes
    lines = [own] + [move(own, sizes, 0, r) for r in range(1, nz)]
    first = jnp.stack([line[:cut] for line in lines])
    second = jnp.stack([line[cut:] for line in lines])
    first_x = [first] + [move(first, sizes, 2, r) for r in range(1, nx)]
    second_y = [second] + [move(second, sizes, 1, r) for r in range(1, ny)]
    first_all = [[part] + [move(part, sizes, 1, r) for r in range(1, ny)] for part in first_x]
    by_y = [[part] + [move(part, sizes, 2, r) for r in range(1, nx)] for part in second_y]
    second_all = [[by_y[dy][dx] for dy in range(ny)] for dx in range(nx)]
    return first_all, second_all


def scatter_first(keep, sends, sizes):
    got = [move(part, sizes, 1, dy + 1) for dy, part in enumerate(sends)]
    sums = [keep[dx] + sum(part[dx].astype(f32) for part in got) for dx in range(sizes[2])]
    return sums[0] + sum(
        move(sums[dx].astype(bf16), sizes, 2, dx).astype(f32) for dx in range(1, sizes[2])
    )


def scatter_second(keep, sends, sizes):
    got = [move(part, sizes, 2, dx + 1) for dx, part in enumerate(sends)]
    sums = [keep[dy] + sum(part[dy].astype(f32) for part in got) for dy in range(sizes[1])]
    return sums[0] + sum(
        move(sums[dy].astype(bf16), sizes, 1, dy).astype(f32) for dy in range(1, sizes[1])
    )


def scatter_lines(first, second, sizes):
    def whole(r):
        return jnp.concatenate([first[r], second[r]], axis=0)

    total = whole(0)
    for r in range(1, sizes[0]):
        total = total + move(whole(r).astype(bf16), sizes, 0, r).astype(f32)
    return total


def cost(flops, bytes_accessed, transcendentals=0):
    return pl.CostEstimate(
        flops=int(flops), bytes_accessed=int(bytes_accessed), transcendentals=int(transcendentals)
    )


def params(dims):
    return pltpu.CompilerParams(
        dimension_semantics=("arbitrary",) * dims, vmem_limit_bytes=VMEM_LIMIT
    )


def regroup_matrix(masked=None):
    side = BLOCK * HORIZON
    row = lax.broadcasted_iota(jnp.int32, (side, side), 0)
    column = lax.broadcasted_iota(jnp.int32, (side, side), 1)
    picked = column == (row % BLOCK) * HORIZON + row // BLOCK
    value = picked.astype(f32)
    if masked is not None:
        value = value * masked
    return value.astype(bf16)


def to_time_body(features_ref, grads_ref, mask_ref, features_out, grads_out):
    channels = features_ref.shape[1]
    moved = jnp.dot(regroup_matrix(), features_ref[...], preferred_element_type=f32)
    features_out[...] = moved.astype(bf16).reshape(HORIZON, BLOCK, channels)
    moved = jnp.dot(
        regroup_matrix(mask_ref[0].astype(f32)), grads_ref[...], preferred_element_type=f32
    )
    grads_out[...] = moved.astype(bf16).reshape(HORIZON, BLOCK, channels)


def to_time(features, grads, mask):
    frames, channels = features.shape
    samples = frames // HORIZON
    steps = samples // BLOCK
    side = BLOCK * HORIZON
    rows = pl.BlockSpec((side, channels), lambda b: (b, 0))
    out = pl.BlockSpec((HORIZON, BLOCK, channels), lambda b: (0, b, 0))
    shape = jax.ShapeDtypeStruct((HORIZON, samples, channels), bf16)
    return pl.pallas_call(
        to_time_body,
        grid=(steps,),
        in_specs=[rows, rows, pl.BlockSpec((1, 1, side), lambda b: (b, 0, 0))],
        out_specs=[out, out],
        out_shape=[shape, shape],
        compiler_params=params(1),
        cost_estimate=cost(4 * frames * side * channels, 8 * frames * channels),
        name="to_time",
    )(features, grads, mask.reshape(steps, 1, side))


def from_time_body(place_ref, *refs):
    pieces, out = refs[:-1], refs[-1]
    count, width = len(pieces), pieces[0].shape[2]
    for r, piece in enumerate(pieces):
        rows = piece[...].reshape(HORIZON * BLOCK, width)
        moved = jnp.dot(regroup_matrix(), rows, preferred_element_type=f32).astype(bf16)
        column = pl.multiple_of(((place_ref[3] + count - r) % count) * width, width)
        out[:, pl.ds(column, width)] = moved


def from_time(place, pieces):
    horizon, samples, width = pieces[0].shape
    channels = width * len(pieces)
    frames = horizon * samples
    return pl.pallas_call(
        from_time_body,
        grid_spec=pltpu.PrefetchScalarGridSpec(
            num_scalar_prefetch=1,
            grid=(samples // BLOCK,),
            in_specs=[pl.BlockSpec((HORIZON, BLOCK, width), lambda b, _: (0, b, 0))] * len(pieces),
            out_specs=pl.BlockSpec((HORIZON * BLOCK, channels), lambda b, _: (b, 0)),
        ),
        out_shape=jax.ShapeDtypeStruct((frames, channels), bf16),
        compiler_params=params(1),
        cost_estimate=cost(2 * frames * 256 * channels, 4 * frames * channels),
        name="from_time",
    )(place, *pieces)


def turn_body(sizes, rows, place_ref, *refs):
    pieces, out = refs[:-1], refs[-1]
    count, width = len(pieces), pieces[0].shape[2]
    nz, ny, nx = sizes
    for r, piece in enumerate(pieces):
        shard = (place_ref[3] + count - r) % count
        for tile in range(width // GROUP):
            block = piece[:, :, tile * GROUP : (tile + 1) * GROUP]
            turned = block.reshape(-1, GROUP).T
            for j in range(GROUP // rows):
                owner = shard * (width // rows) + tile * (GROUP // rows) + j
                oz, oy, ox = coordinates(owner, sizes)
                dz = (oz - place_ref[0] + nz) % nz
                dy = (oy - place_ref[1] + ny) % ny
                dx = (ox - place_ref[2] + nx) % nx
                out[pl.ds((dx * ny + dy) * nz + dz, 1)] = turned[j * rows : (j + 1) * rows][None]


def turn(place, pieces, sizes):
    horizon, samples, width = pieces[0].shape
    count = sizes[0] * sizes[1] * sizes[2]
    channels = width * len(pieces)
    rows = channels // count
    frames = horizon * samples
    return pl.pallas_call(
        functools.partial(turn_body, sizes, rows),
        in_specs=[pl.BlockSpec(memory_space=pltpu.SMEM)]
        + [pl.BlockSpec(memory_space=pltpu.VMEM)] * len(pieces),
        out_specs=pl.BlockSpec(memory_space=pltpu.VMEM),
        out_shape=jax.ShapeDtypeStruct((count, rows, frames), bf16),
        compiler_params=pltpu.CompilerParams(vmem_limit_bytes=VMEM_LIMIT),
        cost_estimate=cost(0, 4 * frames * channels),
        name="turn",
    )(place, *pieces)


def zero_ends(padded):
    rows, channels = padded.shape
    edge = rows * HALF // (HORIZON + 2 * HALF)
    zeros = jnp.zeros((edge, channels), padded.dtype)
    padded[:edge] = zeros
    padded[rows - edge :] = zeros


def weight_copies(sizes, cut, place_ref, firsts, seconds, weight, sems):
    nz, ny, nx = sizes
    rows = firsts[0].shape[2]
    copies = []
    for start, taps, pieces in ((0, cut, firsts), (cut, KERNEL - cut, seconds)):
        for dx in range(nx):
            for dy in range(ny):
                for r in range(nz):
                    owner = flat(
                        (
                            (place_ref[0] - r + nz) % nz,
                            (place_ref[1] - dy + ny) % ny,
                            (place_ref[2] - dx + nx) % nx,
                        ),
                        sizes,
                    )
                    at = pl.ds(pl.multiple_of(owner * rows, rows), rows)
                    copies.append(
                        pltpu.make_async_copy(
                            pieces[dx * ny + dy].at[r],
                            weight.at[pl.ds(start, taps), at, :],
                            sems.at[len(copies)],
                        )
                    )
    return copies


def column_copies(place_ref, pieces, target, sems, first_sem):
    count, width = len(pieces), pieces[0].shape[-1]
    copies = []
    for r, piece in enumerate(pieces):
        column = pl.multiple_of(((place_ref[3] + count - r) % count) * width, width)
        copies.append(
            pltpu.make_async_copy(
                piece, target.at[..., pl.ds(column, width)], sems.at[first_sem + r]
            )
        )
    return copies


def blocks_of(samples, body):
    def step(b, carry):
        body(pl.ds(pl.multiple_of(b * BLOCK, BLOCK), BLOCK))
        return carry

    lax.fori_loop(0, samples // BLOCK, step, 0)


def group_mean(value):
    return jnp.sum(jnp.sum(value, axis=0), axis=1, keepdims=True)[None] / (HORIZON * GROUP)


def norm_of(a):
    centre = a - group_mean(a)
    spread = lax.rsqrt(group_mean(centre * centre) + EPSILON)
    return centre * spread, spread


def norm_back(h, unit, spread):
    return spread * (h - group_mean(h) - unit * group_mean(h * unit))


def conv_front(sizes, cut, place_ref, inputs, firsts, seconds, quarters, padded, weight, acc, sems):
    n, k = pl.program_id(0), pl.program_id(1)
    samples = acc.shape[1]
    tile = acc.shape[2]
    frames = HORIZON * samples
    height = weight.shape[1] // len(quarters)

    def out_copies():
        count = len(quarters)
        base = len(firsts) * sizes[0] * 2 + len(inputs)
        return [
            pltpu.make_async_copy(
                weight.at[:, pl.ds(pl.multiple_of(((place_ref[3] + r) % count) * height, height), height), :],
                quarter,
                sems.at[base + r],
            )
            for r, quarter in enumerate(quarters)
        ]

    @pl.when((n == 0) & (k == 0))
    def _():
        copies = weight_copies(sizes, cut, place_ref, firsts, seconds, weight, sems)
        copies += column_copies(
            place_ref, inputs, padded.at[pl.ds(HALF * samples, frames)], sems, len(copies)
        )
        for copy in copies:
            copy.start()
        zero_ends(padded)
        for copy in copies:
            copy.wait()
        for copy in out_copies():
            copy.start()

    rows = padded[pl.ds(pl.multiple_of(k * samples, BLOCK), frames), :]
    columns = weight[k, :, pl.ds(pl.multiple_of(n * tile, tile), tile)]
    part = jnp.dot(rows, columns, preferred_element_type=f32).reshape(acc.shape)

    @pl.when(k == 0)
    def _():
        acc[...] = part

    @pl.when(k > 0)
    def _():
        acc[...] += part

    @pl.when((n == pl.num_programs(0) - 1) & (k == KERNEL - 1))
    def _():
        for copy in out_copies():
            copy.wait()


def first_body(sizes, cut, shards, place_ref, *refs):
    count = sizes[1] * sizes[2]
    inputs, firsts, seconds = refs[:1], refs[1 : 1 + count], refs[1 + count : 1 + 2 * count]
    scale, shifting, gain, shift = refs[1 + 2 * count : 5 + 2 * count]
    unit_out, spread_out, lifted_out = refs[5 + 2 * count : 8 + 2 * count]
    quarters = refs[8 + 2 * count : 8 + 2 * count + shards]
    padded, weight, acc, sems = refs[8 + 2 * count + shards :]
    conv_front(sizes, cut, place_ref, inputs, firsts, seconds, quarters, padded, weight, acc, sems)

    @pl.when(pl.program_id(1) == KERNEL - 1)
    def _():
        for group in range(acc.shape[2] // GROUP):
            lanes = pl.ds(group * GROUP, GROUP)

            def body(at, group=group, lanes=lanes):
                unit, spread = norm_of(acc[:, at, lanes])
                unit_out[:, at, lanes] = unit
                spread_out[group, at, :] = jnp.broadcast_to(spread[0], (BLOCK, GROUP))
                mixed = mish_act(unit * gain[:, lanes][None] + shift[:, lanes][None])
                lifted = scale[at, lanes][None] * mixed + shifting[at, lanes][None]
                lifted_out[:, at, lanes] = lifted.astype(bf16)

            blocks_of(acc.shape[1], body)


def second_body(sizes, cut, shards, place_ref, *refs):
    count = sizes[1] * sizes[2]
    inputs, refs = refs[:shards], refs[shards:]
    firsts, seconds = refs[:count], refs[count : 2 * count]
    features, upstream, gain, shift = refs[2 * count : 4 + 2 * count]
    block_out, grad_out, sums_out = refs[4 + 2 * count : 7 + 2 * count]
    quarters = refs[7 + 2 * count : 7 + 2 * count + shards]
    padded, weight, acc, sems = refs[7 + 2 * count + shards :]
    conv_front(sizes, cut, place_ref, inputs, firsts, seconds, quarters, padded, weight, acc, sems)

    @pl.when(pl.program_id(1) == KERNEL - 1)
    def _():
        sums_out[...] = jnp.zeros_like(sums_out)
        for group in range(acc.shape[2] // GROUP):
            lanes = pl.ds(group * GROUP, GROUP)

            def body(at, lanes=lanes):
                unit, spread = norm_of(acc[:, at, lanes])
                gain_here = gain[:, lanes][None]
                normed = unit * gain_here + shift[:, lanes][None]
                w, r, t = mish_parts(normed)
                block = features[:, at, lanes].astype(f32) + normed * t
                block_out[:, at, lanes] = block.astype(bf16)
                slope = t + normed * (4.0 * w * (1.0 + w)) * (r * r)
                grad = upstream[:, at, lanes].astype(f32) * slope
                sums_out[0:1, lanes] += jnp.sum(jnp.sum(grad * unit, axis=0), axis=0, keepdims=True)
                sums_out[1:2, lanes] += jnp.sum(jnp.sum(grad, axis=0), axis=0, keepdims=True)
                grad_out[:, at, lanes] = norm_back(grad * gain_here, unit, spread).astype(bf16)

            blocks_of(acc.shape[1], body)


def conv_call(body, name, place, sizes, cut, inputs, pieces, extras, extra_specs, outs, out_specs):
    shards = lax.axis_size("shard")
    horizon, samples, _ = inputs[0].shape
    channels = inputs[0].shape[2] * len(inputs)
    frames = horizon * samples
    firsts = [part for row in pieces[0] for part in row]
    seconds = [part for row in pieces[1] for part in row]
    width = firsts[0].shape[3]
    tile = min(256, width)
    inputs = [part.reshape(frames, part.shape[2]) for part in inputs]
    quarter = jax.ShapeDtypeStruct((KERNEL, width, width), bf16)
    anywhere = pl.BlockSpec(memory_space=pl.ANY)
    copies = 2 * len(firsts) * sizes[0] + len(inputs) + shards
    return pl.pallas_call(
        functools.partial(body, sizes, cut, shards),
        grid_spec=pltpu.PrefetchScalarGridSpec(
            num_scalar_prefetch=1,
            grid=(width // tile, KERNEL),
            in_specs=[anywhere] * (len(inputs) + 2 * len(firsts)) + extra_specs,
            out_specs=out_specs + [anywhere] * shards,
            scratch_shapes=[
                pltpu.VMEM(((HORIZON + 2 * HALF) * samples, channels), bf16),
                pltpu.VMEM((KERNEL, channels, width), bf16),
                pltpu.VMEM((HORIZON, samples, tile), f32),
                pltpu.SemaphoreType.DMA((copies,)),
            ],
        ),
        out_shape=outs + [quarter] * shards,
        compiler_params=params(2),
        cost_estimate=cost(
            2 * KERNEL * frames * channels * width, 24 * frames * width + 10 * channels * width
        ),
        name=name,
    )(place, *inputs, *firsts, *seconds, *extras)


def back_front(place_ref, grads, quarters, padded, weight, acc, sems):
    n, k = pl.program_id(0), pl.program_id(1)
    samples = acc.shape[1]
    tile = acc.shape[2]
    frames = HORIZON * samples

    @pl.when((n == 0) & (k == 0))
    def _():
        copies = column_copies(
            place_ref, grads, padded.at[pl.ds(HALF * samples, frames)], sems, 0
        )
        copies += column_copies(place_ref, quarters, weight, sems, len(copies))
        for copy in copies:
            copy.start()
        zero_ends(padded)
        for copy in copies:
            copy.wait()

    rows = padded[pl.ds(pl.multiple_of((KERNEL - 1 - k) * samples, BLOCK), frames), :]
    own = weight[k, pl.ds(pl.multiple_of(n * tile, tile), tile), :]
    part = lax.dot_general(rows, own, (((1,), (1,)), ((), ())), preferred_element_type=f32)
    part = part.reshape(acc.shape)

    @pl.when(k == 0)
    def _():
        acc[...] = part

    @pl.when(k > 0)
    def _():
        acc[...] += part


def lifted_back_body(shards, place_ref, *refs):
    grads, quarters, refs = refs[:shards], refs[shards : 2 * shards], refs[2 * shards :]
    unit_in, spread_in, scale, gain, shift = refs[:5]
    grad_out, film_out, sums_out = refs[5:8]
    padded, weight, acc, sems = refs[8:]
    back_front(place_ref, grads, quarters, padded, weight, acc, sems)

    @pl.when(pl.program_id(1) == KERNEL - 1)
    def _():
        sums_out[...] = jnp.zeros_like(sums_out)
        for group in range(acc.shape[2] // GROUP):
            lanes = pl.ds(group * GROUP, GROUP)

            def body(at, group=group, lanes=lanes):
                grad_lifted = acc[:, at, lanes]
                unit = unit_in[:, at, lanes]
                spread = spread_in[group, at, :][None]
                gain_here = gain[:, lanes][None]
                normed = unit * gain_here + shift[:, lanes][None]
                w, r, t = mish_parts(normed)
                film_out[0, at, lanes] = jnp.sum(grad_lifted * (normed * t), axis=0)
                film_out[1, at, lanes] = jnp.sum(grad_lifted, axis=0)
                slope = t + normed * (4.0 * w * (1.0 + w)) * (r * r)
                grad = grad_lifted * scale[at, lanes][None] * slope
                sums_out[0:1, lanes] += jnp.sum(jnp.sum(grad * unit, axis=0), axis=0, keepdims=True)
                sums_out[1:2, lanes] += jnp.sum(jnp.sum(grad, axis=0), axis=0, keepdims=True)
                grad_out[:, at, lanes] = norm_back(grad * gain_here, unit, spread).astype(bf16)

            blocks_of(acc.shape[1], body)


def features_back_body(shards, place_ref, *refs):
    grads, quarters, refs = refs[:shards], refs[shards : 2 * shards], refs[2 * shards :]
    upstream, grad_out, padded, weight, acc, sems = refs
    back_front(place_ref, grads, quarters, padded, weight, acc, sems)

    @pl.when(pl.program_id(1) == KERNEL - 1)
    def _():
        grad_out[...] = (acc[...] + upstream[...].astype(f32)).astype(bf16)


def back_call(body, name, place, grads, quarters, extras, extra_specs, outs, out_specs):
    shards = len(grads)
    horizon, samples, width = grads[0].shape
    channels = width * shards
    frames = horizon * samples
    tile = min(256, width)
    grads = [part.reshape(frames, width) for part in grads]
    anywhere = pl.BlockSpec(memory_space=pl.ANY)
    return pl.pallas_call(
        functools.partial(body, shards),
        grid_spec=pltpu.PrefetchScalarGridSpec(
            num_scalar_prefetch=1,
            grid=(width // tile, KERNEL),
            in_specs=[anywhere] * (2 * shards) + extra_specs,
            out_specs=out_specs,
            scratch_shapes=[
                pltpu.VMEM(((HORIZON + 2 * HALF) * samples, channels), bf16),
                pltpu.VMEM((KERNEL, width, channels), bf16),
                pltpu.VMEM((HORIZON, samples, tile), f32),
                pltpu.SemaphoreType.DMA((2 * shards,)),
            ],
        ),
        out_shape=outs,
        compiler_params=params(2),
        cost_estimate=cost(
            2 * KERNEL * frames * channels * width, 24 * frames * width + 10 * channels * width
        ),
        name=name,
    )(place, *grads, *quarters, *extras)


def weight_grad_body(sizes, start, along_y, turned, grads, *refs):
    nz, ny, nx = sizes
    padded = refs[-1]
    keep, sends = refs[0], refs[1:-1]
    rows = turned.shape[1]
    frames = turned.shape[2]
    samples = frames // HORIZON
    k = pl.program_id(0)

    @pl.when(k == 0)
    def _():
        zero_ends(padded)
        padded[HALF * samples : HALF * samples + frames, :] = grads[...]

    at = pl.multiple_of((KERNEL - 1 - start - k) * samples, BLOCK)
    lifted = turned[...].reshape(-1, frames)
    part = jnp.dot(lifted, padded[pl.ds(at, frames), :], preferred_element_type=f32)
    part = part.reshape(nx, ny, nz, 1, rows, part.shape[1])
    if along_y:
        keep[...] = part[:, 0]
        for dy, send in enumerate(sends):
            send[...] = part[:, dy + 1].astype(bf16)
    else:
        keep[...] = part[0]
        for dx, send in enumerate(sends):
            send[...] = part[dx + 1].astype(bf16)


def weight_grad(turned, grads, sizes, start, stop, along_y):
    nz, ny, nx = sizes
    count, rows, frames = turned.shape
    horizon, samples, width = grads.shape
    kept, sent = (nx, ny) if along_y else (ny, nx)
    block = pl.BlockSpec((kept, nz, 1, rows, width), lambda k: (0, 0, k, 0, 0))
    shape = (kept, nz, stop - start, rows, width)
    whole = pl.BlockSpec(memory_space=pltpu.VMEM)
    result = pl.pallas_call(
        functools.partial(weight_grad_body, sizes, start, along_y),
        grid=(stop - start,),
        in_specs=[whole, whole],
        out_specs=[block] * sent,
        out_shape=[jax.ShapeDtypeStruct(shape, f32)]
        + [jax.ShapeDtypeStruct(shape, bf16)] * (sent - 1),
        scratch_shapes=[pltpu.VMEM(((HORIZON + 2 * HALF) * samples, width), bf16)],
        compiler_params=params(1),
        cost_estimate=cost(
            2 * (stop - start) * count * rows * frames * width,
            2 * count * rows * frames + 6 * (stop - start) * count * rows * width,
        ),
        name="weight_grad",
    )(turned, grads.reshape(frames, width))
    return result[0], list(result[1:])


def conv_weight_grad(turned, grads, sizes, cut):
    first = scatter_first(*weight_grad(turned, grads, sizes, 0, cut, True), sizes)
    second = scatter_second(*weight_grad(turned, grads, sizes, cut, KERNEL, False), sizes)
    return scatter_lines(first, second, sizes)


def local(
    features,
    condition,
    task_ids,
    conv_first,
    conv_second,
    film_weight,
    norm_gain_first,
    norm_shift_first,
    norm_gain_second,
    norm_shift_second,
    film_bias,
    task_table,
    out_grad,
    grad_mask,
):
    count, shards = lax.axis_size("dp"), lax.axis_size("shard")
    sizes = digits(count)
    nz, ny, nx = sizes
    me, own = lax.axis_index("dp"), lax.axis_index("shard")
    position = coordinates(me, sizes)
    place = jnp.stack([position[0], position[1], position[2], own]).astype(jnp.int32)
    samples = condition.shape[0]
    channels = features.shape[1]
    width = channels // shards
    tile = min(256, width)
    film_rows, film_width = film_weight.shape

    def own_columns(value, each):
        return lax.dynamic_slice_in_dim(value, own * each, each, value.ndim - 1)

    vectors = jnp.concatenate(
        [norm_gain_first, norm_shift_first, norm_gain_second, norm_shift_second, film_bias]
    )
    each = norm_gain_first.shape[0]
    block = jnp.pad(vectors, (0, 2048 - vectors.shape[0])).reshape(16, 128)
    everyone = lax.all_gather(block, ("dp", "shard"), axis=0, tiled=False).astype(f32)
    everyone = everyone.reshape(count * shards, 2048)
    gain_a, shift_a, gain_b, shift_b = [
        own_columns(everyone[:, i * each : (i + 1) * each].reshape(1, -1), width) for i in range(4)
    ]
    bias = everyone[:, 4 * each : 6 * each].reshape(1, -1)

    cond_in = condition.astype(f32)
    onehot = (task_ids[:, None] == jnp.arange(task_table.shape[0])[None, :]).astype(bf16)
    cond_in = cond_in + jnp.dot(onehot, task_table, preferred_element_type=f32)
    embedded = mish_act(cond_in).astype(bf16)

    offsets = [(dx, dy, r) for dx in range(nx) for dy in range(ny) for r in range(nz)]

    def around_me(sign):
        return jnp.stack(
            [
                flat(
                    (
                        (position[0] + sign * r) % nz,
                        (position[1] + sign * dy) % ny,
                        (position[2] + sign * dx) % nx,
                    ),
                    sizes,
                )
                for dx, dy, r in offsets
            ]
        )

    def ordered(value, order):
        return value.reshape(-1, count, film_rows)[:, order].reshape(-1, count * film_rows)

    behind, ahead = around_me(-1), around_me(1)
    film_cut = film_rows // 32 * 16 if film_rows >= 32 else film_rows // 2
    film_first, film_second = gather_pieces(film_weight, film_cut, sizes)
    film_all = jnp.concatenate(
        [
            jnp.concatenate([film_first[dx][dy], film_second[dx][dy]], axis=1)
            for dx in range(nx)
            for dy in range(ny)
        ]
    ).reshape(count * film_rows, film_width)
    film_own = jnp.dot(ordered(embedded, behind), film_all, preferred_element_type=f32)
    film_own = film_own + own_columns(bias, film_width)
    film_parts = around(film_own)
    order = (own - jnp.arange(shards)) % shards
    film_out = jnp.stack(film_parts)[order]
    film_out = jnp.moveaxis(film_out, 0, 1).reshape(samples, 2 * channels)
    scale = own_columns(film_out[:, :channels], width)
    shifting = own_columns(film_out[:, channels:], width)

    timed, upstream = to_time(features, out_grad, grad_mask)
    turned_a = turn(place, [timed], sizes)
    upstream = own_columns(upstream, width)
    residual = own_columns(timed, width)
    cut_a, cut_b = HALF + 1, HALF
    pieces_a = gather_pieces(conv_first, cut_a, sizes)
    pieces_b = gather_pieces(conv_second, cut_b, sizes)

    column = pl.BlockSpec((samples, tile), lambda n, k, *_: (0, n))
    vector = pl.BlockSpec((1, tile), lambda n, k, *_: (0, n))
    pair = pl.BlockSpec((2, tile), lambda n, k, *_: (0, n))
    field = pl.BlockSpec((HORIZON, samples, tile), lambda n, k, *_: (0, 0, n))
    spreads = pl.BlockSpec((tile // GROUP, samples, GROUP), lambda n, k, *_: (n, 0, 0))
    films = pl.BlockSpec((2, samples, tile), lambda n, k, *_: (0, 0, n))
    field_shape = (HORIZON, samples, width)
    pair_shape = jax.ShapeDtypeStruct((2, width), f32)
    spread_shape = jax.ShapeDtypeStruct((width // GROUP, samples, GROUP), f32)

    unit_a, spread_a, lifted, *quarters_a = conv_call(
        first_body,
        "conv_first",
        place,
        sizes,
        cut_a,
        [timed],
        pieces_a,
        [scale, shifting, gain_a, shift_a],
        [column, column, vector, vector],
        [jax.ShapeDtypeStruct(field_shape, f32), spread_shape, jax.ShapeDtypeStruct(field_shape, bf16)],
        [field, spreads, field],
    )
    lifted_all = around(lifted)
    turned_b = turn(place, lifted_all, sizes)
    block_own, grad_second, sums_b, *quarters_b = conv_call(
        second_body,
        "conv_second",
        place,
        sizes,
        cut_b,
        lifted_all,
        pieces_b,
        [residual, upstream, gain_b, shift_b],
        [field, field, vector, vector],
        [jax.ShapeDtypeStruct(field_shape, bf16), jax.ShapeDtypeStruct(field_shape, bf16), pair_shape],
        [field, field, pair],
    )
    quarters_a = [quarters_a[0]] + [swap(quarters_a[r], r) for r in range(1, shards)]
    quarters_b = [quarters_b[0]] + [swap(quarters_b[r], r) for r in range(1, shards)]
    block_out = from_time(place, around(block_own))

    grad_conv_second = conv_weight_grad(turned_b, grad_second, sizes, cut_b)
    grad_first, grad_film, sums_a = back_call(
        lifted_back_body,
        "lifted_back",
        place,
        around(grad_second),
        quarters_b,
        [unit_a, spread_a, scale, gain_a, shift_a],
        [field, spreads, column, vector, vector],
        [
            jax.ShapeDtypeStruct(field_shape, bf16),
            jax.ShapeDtypeStruct((2, samples, width), f32),
            pair_shape,
        ],
        [field, films, pair],
    )
    grad_conv_first = conv_weight_grad(turned_a, grad_first, sizes, cut_a)
    grad_features_own = back_call(
        features_back_body,
        "features_back",
        place,
        around(grad_first),
        quarters_a,
        [upstream],
        [field],
        jax.ShapeDtypeStruct(field_shape, bf16),
        field,
    )
    grad_features = from_time(place, around(grad_features_own))

    low_parts = jnp.stack(around(grad_film.astype(bf16)))[order]
    low = jnp.moveaxis(low_parts, 0, 2).reshape(2, samples, channels)
    low = jnp.moveaxis(low, 0, 1).reshape(samples, 2 * channels)
    low_own = own_columns(low, film_width)
    film_grad = lax.dot_general(
        ordered(embedded, ahead), low_own, (((0,), (0,)), ((), ())), preferred_element_type=f32
    ).reshape(nx, ny, nz, film_rows, film_width)
    part = film_grad[:, :, :, :film_cut]
    first = scatter_first(
        part[:, 0], [part[:, dy].astype(bf16) for dy in range(1, ny)], sizes
    )
    part = film_grad[:, :, :, film_cut:]
    second = scatter_second(part[0], [part[dx].astype(bf16) for dx in range(1, nx)], sizes)
    grad_film_weight = scatter_lines(first, second, sizes)

    grad_embedded = lax.dot_general(
        low_own, film_all, (((1,), (1,)), ((), ())), preferred_element_type=f32
    )
    grad_cond = grad_embedded * mish_slope(ordered(cond_in, behind))
    grad_table = lax.dot_general(
        onehot.astype(f32), grad_cond, (((0,), (0,)), ((), ())), precision=lax.Precision.HIGHEST
    )
    inverse = jnp.zeros((count,), behind.dtype).at[behind].set(jnp.arange(count))
    grad_table = ordered(grad_table, inverse)

    sums = jnp.concatenate([sums_a, sums_b, jnp.sum(grad_film, axis=1)])
    sums = lax.dynamic_update_slice(jnp.zeros((6, channels), f32), sums, (0, own * width)).reshape(-1)
    condition_width = grad_table.shape[1]
    sum_rows = -(-sums.shape[0] // condition_width)
    sums = jnp.pad(sums, (0, sum_rows * condition_width - sums.shape[0]))
    total = jnp.concatenate([grad_table, sums.reshape(sum_rows, condition_width)])
    total = lax.psum(total, ("dp", "shard"))
    task_count = grad_table.shape[0]
    grad_table = total[:task_count]
    sums = total[task_count:].reshape(-1)[: 6 * channels].reshape(6, channels)
    index = me * shards + own
    small = [lax.dynamic_slice(sums[i], (index * each,), (each,)) for i in range(4)]
    grad_film_bias = lax.dynamic_slice(sums[4:].reshape(-1), (index * 2 * each,), (2 * each,))
    return (
        block_out,
        grad_features,
        grad_conv_first,
        grad_conv_second,
        grad_film_weight,
        small[0],
        small[1],
        small[2],
        small[3],
        grad_film_bias,
        grad_table,
    )


def solution(mesh):
    return jax.shard_map(
        local,
        mesh=mesh,
        in_specs=(
            P("dp", None),
            P("dp", None),
            P("dp"),
            P(None, "dp", "shard"),
            P(None, "dp", "shard"),
            P("dp", "shard"),
            P(("dp", "shard")),
            P(("dp", "shard")),
            P(("dp", "shard")),
            P(("dp", "shard")),
            P(("dp", "shard")),
            P(),
            P("dp", None),
            P("dp"),
        ),
        out_specs=(
            P("dp", None),
            P("dp", None),
            P(None, "dp", "shard"),
            P(None, "dp", "shard"),
            P("dp", "shard"),
            P(("dp", "shard")),
            P(("dp", "shard")),
            P(("dp", "shard")),
            P(("dp", "shard")),
            P(("dp", "shard")),
            P(),
        ),
        check_vma=False,
    )
```

time: 1260 us -> 687 us (0.55)
  local copies, waits for them, and re-layouts: 341 us -> 65.8 us
  waiting for transfers between devices: 565 us -> 313 us
  Pallas kernels: 0 us -> 147 us
  matrix products: 152 us -> 7.3 us
  starting transfers between devices: 0.39 us -> 58.7 us
  blocking collectives: 108 us -> 49.7 us
  other arithmetic: 64 us -> 28.4 us
    reduce_scatter x3 -> x0, waiting for transfers between devices: 377 us -> none  [the longest x1 226 us: backward(): lax.psum_scatter(grad_conv_a, 'dp', scatter_dimension=1, tiled=True)]
    ppermute x0 -> x57, waiting for transfers between devices: none -> 193 us  [the longest x48 193 us: move(): return lax.ppermute(value, 'dp', pairs)]
    all_gather x6 -> x0, waiting for transfers between devices: 186 us -> none  [the longest x1 85.7 us: fetch_weights(): lax.all_gather(conv_first, 'dp', axis=1, tiled=True)]
    pallas_call x0 -> x13, Pallas kernels: none -> 147 us  [the longest x2 53.7 us: conv_call(): pl.pallas_call(functools.partial(body, sizes, cut, shards), grid_spec=plt...]
    dot_general x11 -> x5, matrix products: 152 us -> 7.3 us  [the longest x1 2.74 us: local(): lax.dot_general(low_own, film_all, (((1,), (1,)), ((), ())), preferred_el...]
    psum x1, waiting for transfers between devices: 0.01 us -> 119 us  [local(): total = lax.psum(total, ('dp', 'shard'))]
    unnamed x2 -> x0, blocking collectives: 108 us -> none
    another operation x8 -> x27, local copies, waits for them, and re-layouts: 106 us -> 10.5 us  [the longest x12 6.76 us: gather_pieces(): first = jnp.stack([line[:cut] for line in lines])]
  transfers between devices with their start and end apart: 10 -> 58, of which waited for: 6 -> 24; matrix products, arithmetic and copies ran while one was open for 30% -> 13% of each run, Pallas kernels for 0% -> 15%
where the time goes in v1:
time: 687 us; the launch traced here: 684 us
  waiting for transfers between devices  313 us (46%)
  Pallas kernels  147 us (21%)
  local copies, waits for them, and re-layouts  65.8 us (10%)
  starting transfers between devices  58.7 us (9%)
  blocking collectives  49.7 us (7%)
  other arithmetic  28.4 us (4%)
  between operations  15.2 us (2%)
  matrix products  7.3 us (1%)
    ppermute x48, waiting for transfers between devices, move(): return lax.ppermute(value, 'dp', pairs)  193 us
    psum x1, waiting for transfers between devices, local(): total = lax.psum(total, ('dp', 'shard'))  119 us
    ppermute x48, starting transfers between devices, move(): return lax.ppermute(value, 'dp', pairs)  57.8 us
    pallas_call x2, Pallas kernels, conv_call(): pl.pallas_call(functools.partial(body, sizes, cut, shards), grid_spec=plt...  53.7 us
    all_gather x1, blocking collectives, local(): lax.all_gather(block, ('dp', 'shard'), axis=0, tiled=False).astype(f32)  49.7 us
    pallas_call x2, Pallas kernels, back_call(): pl.pallas_call(functools.partial(body, shards), grid_spec=pltpu.PrefetchS...  39.5 us
    pallas_call x4, Pallas kernels, weight_grad(): pl.pallas_call(functools.partial(weight_grad_body, sizes, start, along_y)...  28.8 us
  transfers between devices with their start and end apart: 58, of which 24 were waited for; matrix products, arithmetic and copies ran while one was open for 13% of the time, Pallas kernels for 15%

profile of v1, /device:TPU:10, one launch (start us, length us, event | category | flops | bytes accessed | tf_op | source)
XLA Modules:
  0.0 684.3 jit_solution(16843592184807509897)
XLA Ops:
  16.1 3.4 concatenate.112
  19.5 49.7 %all_gather.3 = bf16[32,16,128]{2,1,0:T(8,128)(2,1)S(1)} all-gather(bf16[1,16,128]{2,1,0:T(8,128)(2,1)S(1)} %pad_bitcast_fusion), channel_id=1, replica_groups=mesh['dp'=16,'shard'=2] {'dp','shard'}, dimensions={0}, use_global_device_ids=true | all-gather | bytes 135168 | tf_op jit(solution)/shard_map/all_gather | solution.py:643
  77.1 7.0 %to_time.1 = (bf16[16,96,1024]{2,1,0:T(8,128)(2,1)S(1)}, bf16[16,96,1024]{2,1,0:T(8,128)(2,1)}) custom-call(bf16[1536,1024]{1,0:T(8,128)(2,1)} %features_ref.1, bf16[1536,1024]{1,0:T(8,128)(2,1)} %grads_ref.1, s32[6,1,256]{2,1,0:T(1,128)S(1)} %reshape.1453.mask_ref), custom_call_target="tpu_custom_call" | custom-call | flops 1610612736 | bytes 12582912 | tf_op jit(solution)/shard_map/to_time/pallas_call | solution.py:152
  84.1 3.2 collective-permute-start
  90.5 19.0 %collective-permute-done = bf16[5,64,512]{2,1,0:T(8,128)(2,1)S(1)} collective-permute-done((bf16[5,64,512]{2,1,0:T(8,128)(2,1)S(1)}, bf16[5,64,512]{2,1,0:T(8,128)(2,1)S(1)}, u32[]{:S(2)}, u32[]{:S(2)}) %collective-permute-start) | collective-permute-done | bytes 327712 | tf_op jit(solution)/shard_map/ppermute | solution.py:60
  109.7 6.9 %collective-permute-done.14 = bf16[4,32,1024]{2,1,0:T(8,128)(2,1)S(1)} collective-permute-done((bf16[4,32,1024]{2,1,0:T(8,128)(2,1)S(1)}, bf16[4,32,1024]{2,1,0:T(8,128)(2,1)S(1)}, u32[]{:S(2)}, u32[]{:S(2)}) %collective-permute-start.14) | collective-permute-done | bytes 262176 | tf_op jit(solution)/shard_map/ppermute | solution.py:60
  128.7 15.5 %collective-permute-done.4.refs_3_ = bf16[4,3,64,512]{3,2,1,0:T(8,128)(2,1)S(1)} collective-permute-done((bf16[4,3,64,512]{3,2,1,0:T(8,128)(2,1)S(1)}, bf16[4,3,64,512]{3,2,1,0:T(8,128)(2,1)S(1)}, u32[]{:S(2)}, u32[]{:S(2)}) %collective-permute-start.4) | collective-permute-done | bytes 786464 | tf_op jit(solution)/shard_map/ppermute | solution.py:60
  147.8 5.6 collective-permute-done.6.refs_6_
  161.7 3.2 collective-permute-done.8.refs_8_
  164.9 5.3 collective-permute-done.5.refs_4_
  171.4 25.0 %conv_first.1 = (f32[16,96,512]{2,1,0:T(8,128)}, f32[4,96,128]{2,1,0:T(8,128)S(1)}, bf16[16,96,512]{2,1,0:T(8,128)(2,1)}, bf16[5,512,512]{2,1,0:T(8,128)(2,1)}, bf16[5,512,512]{2,1,0:T(8,128)(2,1)}) custom-call(s32[4]{0:T(128)S(1)} %pad_add_fusion.place_ref, bf16[1536,1024]{1,0:T(8,128)(2,1)} %bitcast.270, bf16[4,3,64,512]{3,2,1,0:T(8,128)(2,1)S(1)} %copy-done.8, ...), custom_call_target="tpu_custom_call" | custom-call | flops 8053063680 | bytes 24117248 | tf_op jit(solution)/shard_map/conv_first/pallas_call | solution.py:420
  204.2 10.7 %collective-permute-done.24.refs_4_ = bf16[4,2,64,512]{3,2,1,0:T(8,128)(2,1)} collective-permute-done((bf16[4,2,64,512]{3,2,1,0:T(8,128)(2,1)}, bf16[4,2,64,512]{3,2,1,0:T(8,128)(2,1)}, u32[]{:S(2)}, u32[]{:S(2)}) %collective-permute-start.24) | collective-permute-done | bytes 524320 | tf_op jit(solution)/shard_map/ppermute | solution.py:60
  220.9 4.0 turn.3.turned
  224.8 6.9 %collective-permute-done.27.refs_8_ = bf16[4,3,64,512]{3,2,1,0:T(8,128)(2,1)} collective-permute-done((bf16[4,3,64,512]{3,2,1,0:T(8,128)(2,1)}, bf16[4,3,64,512]{3,2,1,0:T(8,128)(2,1)}, u32[]{:S(2)}, u32[]{:S(2)}) %collective-permute-start.27) | collective-permute-done | bytes 786464 | tf_op jit(solution)/shard_map/ppermute | solution.py:60
  231.7 16.5 %collective-permute-done.28.refs_9_ = bf16[4,3,64,512]{3,2,1,0:T(8,128)(2,1)} collective-permute-done((bf16[4,3,64,512]{3,2,1,0:T(8,128)(2,1)}, bf16[4,3,64,512]{3,2,1,0:T(8,128)(2,1)}, u32[]{:S(2)}, u32[]{:S(2)}) %collective-permute-start.28) | collective-permute-done | bytes 786464 | tf_op jit(solution)/shard_map/ppermute | solution.py:60
  248.2 28.7 %conv_second.1 = (bf16[16,96,512]{2,1,0:T(8,128)(2,1)}, bf16[16,96,512]{2,1,0:T(8,128)(2,1)}, f32[2,512]{1,0:T(2,128)S(1)}, bf16[5,512,512]{2,1,0:T(8,128)(2,1)}, bf16[5,512,512]{2,1,0:T(8,128)(2,1)}) custom-call(s32[4]{0:T(128)S(1)} %pad_add_fusion.place_ref, bf16[1536,512]{1,0:T(8,128)(2,1)} %bitcast.271, bf16[1536,512]{1,0:T(8,128)(2,1)} %bitcast.48.refs_1_, ...), custom_call_target="tpu_custom_call" | custom-call | flops 8053063680 | bytes 24117248 | tf_op jit(solution)/shard_map/conv_second/pallas_call | solution.py:420
  278.3 8.7 %weight_grad.7 = (f32[2,4,3,64,512]{4,3,2,1,0:T(8,128)}, bf16[2,4,3,64,512]{4,3,2,1,0:T(8,128)(2,1)}) custom-call(bf16[16,64,1536]{2,1,0:T(8,128)(2,1)} %turn.3.turned, bf16[1536,512]{1,0:T(8,128)(2,1)S(1)} %bitcast.275), custom_call_target="tpu_custom_call" | custom-call | flops 4831838208 | bytes 12582912 | tf_op jit(solution)/shard_map/weight_grad/pallas_call | solution.py:583
  288.0 5.8 weight_grad.6
  307.7 10.8 %collective-permute-done.42 = bf16[2,4,2,64,512]{4,3,2,1,0:T(8,128)(2,1)} collective-permute-done((bf16[2,4,2,64,512]{4,3,2,1,0:T(8,128)(2,1)S(1)}, bf16[2,4,2,64,512]{4,3,2,1,0:T(8,128)(2,1)}, u32[]{:S(2)}, u32[]{:S(2)}) %collective-permute-start.42) | collective-permute-done | bytes 1048608 | tf_op jit(solution)/shard_map/ppermute | solution.py:60
  326.5 8.1 %collective-permute-done.43 = bf16[4,2,64,512]{3,2,1,0:T(8,128)(2,1)} collective-permute-done((bf16[4,2,64,512]{3,2,1,0:T(8,128)(2,1)}, bf16[4,2,64,512]{3,2,1,0:T(8,128)(2,1)}, u32[]{:S(2)}, u32[]{:S(2)}) %collective-permute-start.43) | collective-permute-done | bytes 524320 | tf_op jit(solution)/shard_map/ppermute | solution.py:60
  338.2 6.5 from_time.2
  344.7 8.5 %collective-permute-done.45 = bf16[4,3,64,512]{3,2,1,0:T(8,128)(2,1)S(1)} collective-permute-done((bf16[4,3,64,512]{3,2,1,0:T(8,128)(2,1)S(1)}, bf16[4,3,64,512]{3,2,1,0:T(8,128)(2,1)S(1)}, u32[]{:S(2)}, u32[]{:S(2)}) %collective-permute-start.45) | collective-permute-done | bytes 786464 | tf_op jit(solution)/shard_map/ppermute | solution.py:60
  362.2 22.2 %lifted_back.1 = (bf16[16,96,512]{2,1,0:T(8,128)(2,1)S(1)}, f32[2,96,512]{2,1,0:T(8,128)S(1)}, f32[2,512]{1,0:T(2,128)S(1)}) custom-call(s32[4]{0:T(128)S(1)} %pad_add_fusion.place_ref, bf16[1536,512]{1,0:T(8,128)(2,1)S(1)} %bitcast.277, bf16[1536,512]{1,0:T(8,128)(2,1)S(1)} %bitcast.278, bf16[5,512,512]{2,1,0:T(8,128)(2,1)} %get-tuple-element.39.refs_2_, ...), custom_call_target="tpu_custom_call" | custom-call | flops 8053063680 | bytes 24117248 | tf_op jit(solution)/shard_map/lifted_back/pallas_call | solution.py:524
  385.2 8.5 %weight_grad.4 = (f32[2,4,3,64,512]{4,3,2,1,0:T(8,128)}, bf16[2,4,3,64,512]{4,3,2,1,0:T(8,128)(2,1)S(1)}) custom-call(bf16[16,64,1536]{2,1,0:T(8,128)(2,1)} %copy-done.4, bf16[1536,512]{1,0:T(8,128)(2,1)S(1)} %bitcast.272), custom_call_target="tpu_custom_call" | custom-call | flops 4831838208 | bytes 12582912 | tf_op jit(solution)/shard_map/weight_grad/pallas_call | solution.py:583
  397.4 5.8 weight_grad.5
  435.1 119.3 %all-reduce.4.cloned.1.call-done = f32[56,1152]{1,0:T(8,128)} async-done(((f32[56,1152]{1,0:T(8,128)}), f32[56,1152]{1,0:T(8,128)}) %all-reduce.4.cloned.1.call-update) | async-done | bytes 258064 | tf_op jit(solution)/shard_map/psum | solution.py:805
  566.3 34.8 %collective-permute-done.53 = bf16[4,40,1024]{2,1,0:T(8,128)(2,1)S(1)} collective-permute-done((bf16[4,40,1024]{2,1,0:T(8,128)(2,1)S(1)}, bf16[4,40,1024]{2,1,0:T(8,128)(2,1)S(1)}, u32[]{:S(2)}, u32[]{:S(2)}) %collective-permute-start.53) | collective-permute-done | bytes 327712 | tf_op jit(solution)/shard_map/ppermute | solution.py:60
  606.8 4.8 collective-permute-done.54
  619.8 17.2 %features_back.1.refs_0_ = bf16[16,96,512]{2,1,0:T(8,128)(2,1)S(1)} custom-call(s32[4]{0:T(128)S(1)} %pad_add_fusion.place_ref, bf16[1536,512]{1,0:T(8,128)(2,1)S(1)} %bitcast.274, bf16[1536,512]{1,0:T(8,128)(2,1)} %bitcast.60.refs_1_, bf16[5,512,512]{2,1,0:T(8,128)(2,1)} %get-tuple-element.44.refs_2_, bf16[5,512,512]{2,1,0:T(8,128)(2,1)} %collective-permute-done.33.refs_3_, ...), custom_call_target="tpu_custom_call" | custom-call | flops 8053063680 | bytes 24117248 | tf_op jit(solution)/shard_map/features_back/pallas_call | solution.py:524
  642.8 20.3 %collective-permute-done.39 = bf16[5,64,512]{2,1,0:T(8,128)(2,1)S(1)} collective-permute-done((bf16[5,64,512]{2,1,0:T(8,128)(2,1)S(1)}, bf16[5,64,512]{2,1,0:T(8,128)(2,1)S(1)}, u32[]{:S(2)}, u32[]{:S(2)}) %collective-permute-start.39) | collective-permute-done | bytes 327712 | tf_op jit(solution)/shard_map/ppermute | solution.py:60
  663.1 6.6 collective-permute-done.40
  672.5 4.3 from_time.3
  (337 shorter events, 166.1 us)
Async XLA Ops:
  7.2 547.2 %all-reduce.4.cloned.1.call-start = ((), (), s32[]{:S(2)}) async-start(), calls=%async_computation | async-start | bytes 516096 | tf_op jit(solution)/shard_map/psum | solution.py:805
  7.3 76.9 %collective-permute-start.11 = (bf16[72,1024]{1,0:T(8,128)(2,1)}, bf16[72,1024]{1,0:T(8,128)(2,1)S(1)}, u32[]{:S(2)}, u32[]{:S(2)}) collective-permute-start(bf16[72,1024]{1,0:T(8,128)(2,1)} %param.19), channel_id=1, source_target_pairs={{0,24},{2,26},{4,28},{6,30},{8,0},{10,2},{12,4},{14,6},{16,8},{18,... | collective-permute-start | bytes 442376 | tf_op jit(solution)/shard_map/ppermute | solution.py:60
  7.8 79.6 %collective-permute-start.10 = (bf16[72,1024]{1,0:T(8,128)(2,1)}, bf16[72,1024]{1,0:T(8,128)(2,1)S(1)}, u32[]{:S(2)}, u32[]{:S(2)}) collective-permute-start(bf16[72,1024]{1,0:T(8,128)(2,1)} %param.19), channel_id=1, source_target_pairs={{0,16},{2,18},{4,20},{6,22},{8,24},{10,26},{12,28},{14,30},{16,0},... | collective-permute-start | bytes 442376 | tf_op jit(solution)/shard_map/ppermute | solution.py:60
  10.4 77.1 %collective-permute-start.9 = (bf16[72,1024]{1,0:T(8,128)(2,1)}, bf16[72,1024]{1,0:T(8,128)(2,1)S(1)}, u32[]{:S(2)}, u32[]{:S(2)}) collective-permute-start(bf16[72,1024]{1,0:T(8,128)(2,1)} %param.19), channel_id=1, source_target_pairs={{0,8},{2,10},{4,12},{6,14},{8,16},{10,18},{12,20},{14,22},{16,24},... | collective-permute-start | bytes 442376 | tf_op jit(solution)/shard_map/ppermute | solution.py:60
  12.8 77.2 %collective-permute-start.2 = (bf16[5,64,512]{2,1,0:T(8,128)(2,1)}, bf16[5,64,512]{2,1,0:T(8,128)(2,1)S(1)}, u32[]{:S(2)}, u32[]{:S(2)}) collective-permute-start(bf16[5,64,512]{2,1,0:T(8,128)(2,1)} %param.17), channel_id=1, source_target_pairs={{0,24},{2,26},{4,28},{6,30},{8,0},{10,2},{12,4},{14,6},{16,8},{18,... | collective-permute-start | bytes 983048 | tf_op jit(solution)/shard_map/ppermute | solution.py:60
  12.8 77.5 %collective-permute-start.1 = (bf16[5,64,512]{2,1,0:T(8,128)(2,1)}, bf16[5,64,512]{2,1,0:T(8,128)(2,1)S(1)}, u32[]{:S(2)}, u32[]{:S(2)}) collective-permute-start(bf16[5,64,512]{2,1,0:T(8,128)(2,1)} %param.17), channel_id=1, source_target_pairs={{0,16},{2,18},{4,20},{6,22},{8,24},{10,26},{12,28},{14,30},{16,0},... | collective-permute-start | bytes 983048 | tf_op jit(solution)/shard_map/ppermute | solution.py:60
  87.5 29.5 %collective-permute-start.21 = (bf16[5,64,512]{2,1,0:T(8,128)(2,1)}, bf16[5,64,512]{2,1,0:T(8,128)(2,1)S(1)}, u32[]{:S(2)}, u32[]{:S(2)}) collective-permute-start(bf16[5,64,512]{2,1,0:T(8,128)(2,1)} %param.18), channel_id=1, source_target_pairs={{0,16},{2,18},{4,20},{6,22},{8,24},{10,26},{12,28},{14,30},{16,0},... | collective-permute-start | bytes 983048 | tf_op jit(solution)/shard_map/ppermute | solution.py:60
  90.3 31.2 %collective-permute-start.15 = (bf16[4,40,1024]{2,1,0:T(8,128)(2,1)S(1)}, bf16[4,40,1024]{2,1,0:T(8,128)(2,1)S(1)}, u32[]{:S(2)}, u32[]{:S(2)}) collective-permute-start(bf16[4,40,1024]{2,1,0:T(8,128)(2,1)S(1)} %pad_maximum_fusion.6), channel_id=1, source_target_pairs={{0,2},{2,0},{4,6},{6,4},{8,10},{10,8},{12,14},{14,12},{16,18},{18,... | collective-permute-start | bytes 983048 | tf_op jit(solution)/shard_map/ppermute | solution.py:60
  121.6 39.2 %collective-permute-start.3 = (bf16[4,3,64,512]{3,2,1,0:T(8,128)(2,1)S(1)}, bf16[4,3,64,512]{3,2,1,0:T(8,128)(2,1)S(1)}, u32[]{:S(2)}, u32[]{:S(2)}) collective-permute-start(bf16[4,3,64,512]{3,2,1,0:T(8,128)(2,1)S(1)} %pad_maximum_fusion.refs_1_), channel_id=1, source_target_pairs={{0,4},{2,6},{4,0},{6,2},{8,12},{10,14},{12,8},{14,10},{16,20},{18,... | collective-permute-start | bytes 2359304 | tf_op jit(solution)/shard_map/ppermute | solution.py:60
  124.6 28.8 %collective-permute-start.6 = (bf16[4,2,64,512]{3,2,1,0:T(8,128)(2,1)S(1)}, bf16[4,2,64,512]{3,2,1,0:T(8,128)(2,1)}, u32[]{:S(2)}, u32[]{:S(2)}) collective-permute-start(bf16[4,2,64,512]{3,2,1,0:T(8,128)(2,1)S(1)} %pad_maximum_fusion.3.refs_5_), channel_id=1, source_target_pairs={{0,4},{2,6},{4,0},{6,2},{8,12},{10,14},{12,8},{14,10},{16,20},{18,... | collective-permute-start | bytes 1572872 | tf_op jit(solution)/shard_map/ppermute | solution.py:60
  127.3 33.5 %collective-permute-start.7 = (bf16[4,2,64,512]{3,2,1,0:T(8,128)(2,1)S(1)}, bf16[4,2,64,512]{3,2,1,0:T(8,128)(2,1)}, u32[]{:S(2)}, u32[]{:S(2)}) collective-permute-start(bf16[4,2,64,512]{3,2,1,0:T(8,128)(2,1)S(1)} %pad_maximum_fusion.3.refs_5_), channel_id=1, source_target_pairs={{0,2},{2,0},{4,6},{6,4},{8,10},{10,8},{12,14},{14,12},{16,18},{18,... | collective-permute-start | bytes 1572872 | tf_op jit(solution)/shard_map/ppermute | solution.py:60
  128.6 26.9 %collective-permute-start.18 = (f32[96,1024]{1,0:T(8,128)S(1)}, f32[96,1024]{1,0:T(8,128)S(1)}, u32[]{:S(2)}, u32[]{:S(2)}) collective-permute-start(f32[96,1024]{1,0:T(8,128)S(1)} %fusion), channel_id=1, source_target_pairs={{0,1},{1,0},{2,3},{3,2},{4,5},{5,4},{6,7},{7,6},{8,9},{9,8},{10,11... | collective-permute-start | bytes 1179656 | tf_op jit(solution)/shard_map/ppermute | solution.py:65
  153.4 48.5 %collective-permute-start.26 = (bf16[4,3,64,512]{3,2,1,0:T(8,128)(2,1)}, bf16[4,3,64,512]{3,2,1,0:T(8,128)(2,1)}, u32[]{:S(2)}, u32[]{:S(2)}) collective-permute-start(bf16[4,3,64,512]{3,2,1,0:T(8,128)(2,1)} %pad_maximum_fusion.2.refs_6_), channel_id=1, source_target_pairs={{0,4},{2,6},{4,0},{6,2},{8,12},{10,14},{12,8},{14,10},{16,20},{18,... | collective-permute-start | bytes 2359304 | tf_op jit(solution)/shard_map/ppermute | solution.py:60
  200.8 30.9 %collective-permute-start.27 = (bf16[4,3,64,512]{3,2,1,0:T(8,128)(2,1)}, bf16[4,3,64,512]{3,2,1,0:T(8,128)(2,1)}, u32[]{:S(2)}, u32[]{:S(2)}) collective-permute-start(bf16[4,3,64,512]{3,2,1,0:T(8,128)(2,1)} %pad_maximum_fusion.2.refs_6_), channel_id=1, source_target_pairs={{0,2},{2,0},{4,6},{6,4},{8,10},{10,8},{12,14},{14,12},{16,18},{18,... | collective-permute-start | bytes 2359304 | tf_op jit(solution)/shard_map/ppermute | solution.py:60
  201.9 46.3 %collective-permute-start.28 = (bf16[4,3,64,512]{3,2,1,0:T(8,128)(2,1)}, bf16[4,3,64,512]{3,2,1,0:T(8,128)(2,1)}, u32[]{:S(2)}, u32[]{:S(2)}) collective-permute-start(bf16[4,3,64,512]{3,2,1,0:T(8,128)(2,1)} %collective-permute-done.26.refs_7_), channel_id=1, source_target_pairs={{0,2},{2,0},{4,6},{6,4},{8,10},{10,8},{12,14},{14,12},{16,18},{18,... | collective-permute-start | bytes 2359304 | tf_op jit(solution)/shard_map/ppermute | solution.py:60
  287.0 37.6 %collective-permute-start.44 = (bf16[2,4,3,64,512]{4,3,2,1,0:T(8,128)(2,1)}, bf16[2,4,3,64,512]{4,3,2,1,0:T(8,128)(2,1)}, u32[]{:S(2)}, u32[]{:S(2)}) collective-permute-start(bf16[2,4,3,64,512]{4,3,2,1,0:T(8,128)(2,1)} %get-tuple-element.53), channel_id=1, source_target_pairs={{0,2},{2,0},{4,6},{6,4},{8,10},{10,8},{12,14},{14,12},{16,18},{18,... | collective-permute-start | bytes 4718600 | tf_op jit(solution)/shard_map/ppermute | solution.py:60
  307.1 31.0 %collective-permute-start.29 = (bf16[16,96,512]{2,1,0:T(8,128)(2,1)}, bf16[16,96,512]{2,1,0:T(8,128)(2,1)}, u32[]{:S(2)}, u32[]{:S(2)}) collective-permute-start(bf16[16,96,512]{2,1,0:T(8,128)(2,1)} %get-tuple-element.37.refs_0_), channel_id=1, source_target_pairs={{0,1},{1,0},{2,3},{3,2},{4,5},{5,4},{6,7},{7,6},{8,9},{9,8},{10,11... | collective-permute-start | bytes 4718600 | tf_op jit(solution)/shard_map/ppermute | solution.py:65
  307.2 55.0 %collective-permute-start.31 = (bf16[5,512,512]{2,1,0:T(8,128)(2,1)}, bf16[5,512,512]{2,1,0:T(8,128)(2,1)}, u32[]{:S(2)}, u32[]{:S(2)}) collective-permute-start(bf16[5,512,512]{2,1,0:T(8,128)(2,1)} %get-tuple-element.40), channel_id=1, source_target_pairs={{0,1},{1,0},{2,3},{3,2},{4,5},{5,4},{6,7},{7,6},{8,9},{9,8},{10,11... | collective-permute-start | bytes 7864328 | tf_op jit(solution)/shard_map/ppermute | solution.py:65
  323.2 296.6 %collective-permute-start.33 = (bf16[5,512,512]{2,1,0:T(8,128)(2,1)}, bf16[5,512,512]{2,1,0:T(8,128)(2,1)}, u32[]{:S(2)}, u32[]{:S(2)}) collective-permute-start(bf16[5,512,512]{2,1,0:T(8,128)(2,1)} %get-tuple-element.45), channel_id=1, source_target_pairs={{0,1},{1,0},{2,3},{3,2},{4,5},{5,4},{6,7},{7,6},{8,9},{9,8},{10,11... | collective-permute-start | bytes 7864328 | tf_op jit(solution)/shard_map/ppermute | solution.py:65
  324.6 36.1 %collective-permute-start.30 = (bf16[16,96,512]{2,1,0:T(8,128)(2,1)}, bf16[16,96,512]{2,1,0:T(8,128)(2,1)S(1)}, u32[]{:S(2)}, u32[]{:S(2)}) collective-permute-start(bf16[16,96,512]{2,1,0:T(8,128)(2,1)} %get-tuple-element.38), channel_id=1, source_target_pairs={{0,1},{1,0},{2,3},{3,2},{4,5},{5,4},{6,7},{7,6},{8,9},{9,8},{10,11... | collective-permute-start | bytes 4718600 | tf_op jit(solution)/shard_map/ppermute | solution.py:65
  355.5 75.0 %collective-permute-start.46 = (bf16[5,64,512]{2,1,0:T(8,128)(2,1)}, bf16[5,64,512]{2,1,0:T(8,128)(2,1)}, u32[]{:S(2)}, u32[]{:S(2)}) collective-permute-start(bf16[5,64,512]{2,1,0:T(8,128)(2,1)} %pad_maximum_fusion.10), channel_id=1, source_target_pairs={{0,8},{2,10},{4,12},{6,14},{8,16},{10,18},{12,20},{14,22},{16,24},... | collective-permute-start | bytes 983048 | tf_op jit(solution)/shard_map/ppermute | solution.py:60
  359.2 71.6 %collective-permute-start.47 = (bf16[5,64,512]{2,1,0:T(8,128)(2,1)}, bf16[5,64,512]{2,1,0:T(8,128)(2,1)}, u32[]{:S(2)}, u32[]{:S(2)}) collective-permute-start(bf16[5,64,512]{2,1,0:T(8,128)(2,1)} %pad_maximum_fusion.11), channel_id=1, source_target_pairs={{0,16},{2,18},{4,20},{6,22},{8,24},{10,26},{12,28},{14,30},{16,0},... | collective-permute-start | bytes 983048 | tf_op jit(solution)/shard_map/ppermute | solution.py:60
  360.7 70.0 %collective-permute-start.48 = (bf16[5,64,512]{2,1,0:T(8,128)(2,1)}, bf16[5,64,512]{2,1,0:T(8,128)(2,1)}, u32[]{:S(2)}, u32[]{:S(2)}) collective-permute-start(bf16[5,64,512]{2,1,0:T(8,128)(2,1)} %pad_maximum_fusion.12), channel_id=1, source_target_pairs={{0,24},{2,26},{4,28},{6,30},{8,0},{10,2},{12,4},{14,6},{16,8},{18,... | collective-permute-start | bytes 983048 | tf_op jit(solution)/shard_map/ppermute | solution.py:60
  427.2 128.0 %collective-permute-start.50 = (bf16[2,4,32,1024]{3,2,1,0:T(8,128)(2,1)}, bf16[2,4,32,1024]{3,2,1,0:T(8,128)(2,1)}, u32[]{:S(2)}, u32[]{:S(2)}) collective-permute-start(bf16[2,4,32,1024]{3,2,1,0:T(8,128)(2,1)} %slice_bitcast_fusion.4), channel_id=1, source_target_pairs={{0,4},{2,6},{4,0},{6,2},{8,12},{10,14},{12,8},{14,10},{16,20},{18,... | collective-permute-start | bytes 1572872 | tf_op jit(solution)/shard_map/ppermute | solution.py:60
  430.5 189.3 %collective-permute-start.32 = (bf16[16,96,512]{2,1,0:T(8,128)(2,1)}, bf16[16,96,512]{2,1,0:T(8,128)(2,1)}, u32[]{:S(2)}, u32[]{:S(2)}) collective-permute-start(bf16[16,96,512]{2,1,0:T(8,128)(2,1)} %copy-done.11), channel_id=1, source_target_pairs={{0,1},{1,0},{2,3},{3,2},{4,5},{5,4},{6,7},{7,6},{8,9},{9,8},{10,11... | collective-permute-start | bytes 4718600 | tf_op jit(solution)/shard_map/ppermute | solution.py:65
  430.7 134.3 %collective-permute-start.37 = (bf16[2,4,2,64,512]{4,3,2,1,0:T(8,128)(2,1)S(1)}, bf16[2,4,2,64,512]{4,3,2,1,0:T(8,128)(2,1)}, u32[]{:S(2)}, u32[]{:S(2)}) collective-permute-start(bf16[2,4,2,64,512]{4,3,2,1,0:T(8,128)(2,1)S(1)} %get-tuple-element.49), channel_id=1, source_target_pairs={{0,2},{2,0},{4,6},{6,4},{8,10},{10,8},{12,14},{14,12},{16,18},{18,... | collective-permute-start | bytes 3145736 | tf_op jit(solution)/shard_map/ppermute | solution.py:60
  430.7 129.2 %collective-permute-start.52 = (bf16[2,4,40,1024]{3,2,1,0:T(8,128)(2,1)}, bf16[2,4,40,1024]{3,2,1,0:T(8,128)(2,1)}, u32[]{:S(2)}, u32[]{:S(2)}) collective-permute-start(bf16[2,4,40,1024]{3,2,1,0:T(8,128)(2,1)} %slice_bitcast_fusion.1), channel_id=1, source_target_pairs={{0,2},{2,0},{4,6},{6,4},{8,10},{10,8},{12,14},{14,12},{16,18},{18,... | collective-permute-start | bytes 1966088 | tf_op jit(solution)/shard_map/ppermute | solution.py:60
  560.0 58.0 %collective-permute-start.35 = (bf16[2,4,3,64,512]{4,3,2,1,0:T(8,128)(2,1)}, bf16[2,4,3,64,512]{4,3,2,1,0:T(8,128)(2,1)S(1)}, u32[]{:S(2)}, u32[]{:S(2)}) collective-permute-start(bf16[2,4,3,64,512]{4,3,2,1,0:T(8,128)(2,1)} %copy-done.14), channel_id=1, source_target_pairs={{0,4},{2,6},{4,0},{6,2},{8,12},{10,14},{12,8},{14,10},{16,20},{18,... | collective-permute-start | bytes 4718600 | tf_op jit(solution)/shard_map/ppermute | solution.py:60
  562.8 38.3 %collective-permute-start.53 = (bf16[4,40,1024]{2,1,0:T(8,128)(2,1)S(1)}, bf16[4,40,1024]{2,1,0:T(8,128)(2,1)S(1)}, u32[]{:S(2)}, u32[]{:S(2)}) collective-permute-start(bf16[4,40,1024]{2,1,0:T(8,128)(2,1)S(1)} %fusion.4), channel_id=1, source_target_pairs={{0,4},{2,6},{4,0},{6,2},{8,12},{10,14},{12,8},{14,10},{16,20},{18,... | collective-permute-start | bytes 983048 | tf_op jit(solution)/shard_map/ppermute | solution.py:60
  637.0 35.4 %collective-permute-start.34 = (bf16[16,96,512]{2,1,0:T(8,128)(2,1)S(1)}, bf16[16,96,512]{2,1,0:T(8,128)(2,1)S(1)}, u32[]{:S(2)}, u32[]{:S(2)}) collective-permute-start(bf16[16,96,512]{2,1,0:T(8,128)(2,1)S(1)} %features_back.1.refs_0_), channel_id=1, source_target_pairs={{0,1},{1,0},{2,3},{3,2},{4,5},{5,4},{6,7},{7,6},{8,9},{9,8},{10,11... | collective-permute-start | bytes 4718600 | tf_op jit(solution)/shard_map/ppermute | solution.py:65
  641.1 28.7 %collective-permute-start.40 = (bf16[5,64,512]{2,1,0:T(8,128)(2,1)S(1)}, bf16[5,64,512]{2,1,0:T(8,128)(2,1)S(1)}, u32[]{:S(2)}, u32[]{:S(2)}) collective-permute-start(bf16[5,64,512]{2,1,0:T(8,128)(2,1)S(1)} %pad_maximum_fusion.8), channel_id=1, source_target_pairs={{0,16},{2,18},{4,20},{6,22},{8,24},{10,26},{12,28},{14,30},{16,0},... | collective-permute-start | bytes 983048 | tf_op jit(solution)/shard_map/ppermute | solution.py:60
  642.4 29.1 %collective-permute-start.41 = (bf16[5,64,512]{2,1,0:T(8,128)(2,1)S(1)}, bf16[5,64,512]{2,1,0:T(8,128)(2,1)S(1)}, u32[]{:S(2)}, u32[]{:S(2)}) collective-permute-start(bf16[5,64,512]{2,1,0:T(8,128)(2,1)S(1)} %pad_maximum_fusion.9), channel_id=1, source_target_pairs={{0,24},{2,26},{4,28},{6,30},{8,0},{10,2},{12,4},{14,6},{16,8},{18,... | collective-permute-start | bytes 983048 | tf_op jit(solution)/shard_map/ppermute | solution.py:60
  (75 other events, 1305.6 us)
Sparse Core Ops, SparseCore 0:
  428.4 126.0 all-reduce.3

commit v2 on v1

v2 whole, which is shorter than its diff:
```python
import functools

import jax
import jax.numpy as jnp
from jax import lax
from jax.experimental import pallas as pl
from jax.experimental.pallas import tpu as pltpu
from jax.sharding import PartitionSpec as P

KERNEL = 5
HALF = KERNEL // 2
HORIZON = 16
GROUP = 128
EPSILON = 1e-05
BLOCK = 16
VMEM_LIMIT = 48 * 1024 * 1024
f32 = jnp.float32
bf16 = jnp.bfloat16


def mish_parts(v):
    w = jnp.exp(jnp.minimum(v, 20.0))
    n = w * (w + 2.0)
    r = 1.0 / (n + 2.0)
    return w, r, n * r


def mish_act(v):
    return v * mish_parts(v)[2]


def mish_slope(v):
    w, r, t = mish_parts(v)
    return t + v * (4.0 * w * (1.0 + w)) * (r * r)


def digits(count):
    bits = count.bit_length() - 1
    small = bits // 3
    return (1 << (bits - 2 * small), 1 << small, 1 << small)


def coordinates(index, sizes):
    _, ny, nx = sizes
    return (index // (ny * nx), (index // nx) % ny, index % nx)


def flat(position, sizes):
    _, ny, nx = sizes
    return (position[0] * ny + position[1]) * nx + position[2]


def move(value, sizes, axis, by):
    count = sizes[0] * sizes[1] * sizes[2]
    pairs = []
    for source in range(count):
        position = list(coordinates(source, sizes))
        position[axis] = (position[axis] + by) % sizes[axis]
        pairs.append((source, flat(position, sizes)))
    return lax.ppermute(value, "dp", pairs)


def swap(value, by):
    count = lax.axis_size("shard")
    return lax.ppermute(value, "shard", [(i, (i + by) % count) for i in range(count)])


def around(value):
    return [value] + [swap(value, r) for r in range(1, lax.axis_size("shard"))]


def trade(value, sizes, axis, mask):
    count = sizes[0] * sizes[1] * sizes[2]
    pairs = []
    for source in range(count):
        position = list(coordinates(source, sizes))
        position[axis] ^= mask
        pairs.append((source, flat(position, sizes)))
    return lax.ppermute(value, "dp", pairs)


def line_groups(sizes):
    nz, ny, nx = sizes
    return [[flat((z, y, x), sizes) for z in range(nz)] for y in range(ny) for x in range(nx)]


def gather_lines(own, cut, sizes):
    lines = lax.all_gather(own, "dp", axis=0, tiled=False, axis_index_groups=line_groups(sizes))
    return lines[:, :cut], lines[:, cut:]


def move_lines(own, cut, sizes):
    lines = [own] + [move(own, sizes, 0, r) for r in range(1, sizes[0])]
    return jnp.stack([line[:cut] for line in lines]), jnp.stack([line[cut:] for line in lines])


def gather_planes(first, second, sizes):
    _, ny, nx = sizes
    first_x = [first] + [move(first, sizes, 2, r) for r in range(1, nx)]
    second_y = [second] + [move(second, sizes, 1, r) for r in range(1, ny)]
    first_all = [[part] + [move(part, sizes, 1, r) for r in range(1, ny)] for part in first_x]
    by_y = [[part] + [move(part, sizes, 2, r) for r in range(1, nx)] for part in second_y]
    return (
        [first_all[dx][dy] for dx in range(nx) for dy in range(ny)],
        [by_y[dy][dx] for dx in range(nx) for dy in range(ny)],
    )


def scatter_planes(keep, sends, sizes, order):
    near, far = order
    got = [move(sends[r], sizes, near, r + 1).astype(f32) for r in range(sizes[near] - 1)]
    sums = [keep[r] + sum(part[r] for part in got) for r in range(sizes[far])]
    total = sums[0]
    for r in range(1, sizes[far]):
        total = total + move(sums[r].astype(bf16), sizes, far, r).astype(f32)
    return total


def scatter_lines(first, second, sizes):
    def whole(r):
        return jnp.concatenate([first[r], second[r]], axis=0)

    total = whole(0)
    for r in range(1, sizes[0]):
        total = total + move(whole(r).astype(bf16), sizes, 0, r).astype(f32)
    return total


def sum_everywhere(value, sizes):
    shards = lax.axis_size("shard")
    own = lax.axis_index("shard")
    rows = value.shape[0] // shards

    def part(r):
        return lax.dynamic_slice_in_dim(value, (own + r) % shards * rows, rows, 0)

    total = part(0)
    for r in range(1, shards):
        total = total + swap(part(r), r)
    for axis in (2, 1, 0):
        mask = 1
        while mask < sizes[axis]:
            total = total + trade(total, sizes, axis, mask)
            mask *= 2
    return in_order(around(total)).reshape(value.shape)


def in_order(parts):
    shards = len(parts)
    own = lax.axis_index("shard")
    if shards == 2:
        mine = own == 0
        return jnp.stack([jnp.where(mine, parts[0], parts[1]), jnp.where(mine, parts[1], parts[0])])
    return jnp.stack(parts)[(own - jnp.arange(shards)) % shards]


def cost(flops, bytes_accessed, transcendentals=0):
    return pl.CostEstimate(
        flops=int(flops), bytes_accessed=int(bytes_accessed), transcendentals=int(transcendentals)
    )


def params(dims):
    return pltpu.CompilerParams(
        dimension_semantics=("arbitrary",) * dims, vmem_limit_bytes=VMEM_LIMIT
    )


def regroup_matrix(masked=None):
    side = BLOCK * HORIZON
    row = lax.broadcasted_iota(jnp.int32, (side, side), 0)
    column = lax.broadcasted_iota(jnp.int32, (side, side), 1)
    picked = column == (row % BLOCK) * HORIZON + row // BLOCK
    value = picked.astype(f32)
    if masked is not None:
        value = value * masked
    return value.astype(bf16)


def to_time_body(features_ref, grads_ref, mask_ref, features_out, grads_out):
    channels = features_ref.shape[1]
    moved = jnp.dot(regroup_matrix(), features_ref[...], preferred_element_type=f32)
    features_out[...] = moved.astype(bf16).reshape(HORIZON, BLOCK, channels)
    moved = jnp.dot(
        regroup_matrix(mask_ref[0].astype(f32)), grads_ref[...], preferred_element_type=f32
    )
    grads_out[...] = moved.astype(bf16).reshape(HORIZON, BLOCK, channels)


def to_time(features, grads, mask):
    frames, channels = features.shape
    samples = frames // HORIZON
    steps = samples // BLOCK
    side = BLOCK * HORIZON
    rows = pl.BlockSpec((side, channels), lambda b: (b, 0))
    out = pl.BlockSpec((HORIZON, BLOCK, channels), lambda b: (0, b, 0))
    shape = jax.ShapeDtypeStruct((HORIZON, samples, channels), bf16)
    return pl.pallas_call(
        to_time_body,
        grid=(steps,),
        in_specs=[rows, rows, pl.BlockSpec((1, 1, side), lambda b: (b, 0, 0))],
        out_specs=[out, out],
        out_shape=[shape, shape],
        compiler_params=params(1),
        cost_estimate=cost(4 * frames * side * channels, 8 * frames * channels),
        name="to_time",
    )(features, grads, mask.reshape(steps, 1, side))


def from_time_body(place_ref, *refs):
    pieces, out = refs[:-1], refs[-1]
    count, width = len(pieces), pieces[0].shape[2]
    for r, piece in enumerate(pieces):
        rows = piece[...].reshape(HORIZON * BLOCK, width)
        moved = jnp.dot(regroup_matrix(), rows, preferred_element_type=f32).astype(bf16)
        column = pl.multiple_of(((place_ref[3] + count - r) % count) * width, width)
        out[:, pl.ds(column, width)] = moved


def from_time(place, pieces):
    horizon, samples, width = pieces[0].shape
    channels = width * len(pieces)
    frames = horizon * samples
    return pl.pallas_call(
        from_time_body,
        grid_spec=pltpu.PrefetchScalarGridSpec(
            num_scalar_prefetch=1,
            grid=(samples // BLOCK,),
            in_specs=[pl.BlockSpec((HORIZON, BLOCK, width), lambda b, _: (0, b, 0))] * len(pieces),
            out_specs=pl.BlockSpec((HORIZON * BLOCK, channels), lambda b, _: (b, 0)),
        ),
        out_shape=jax.ShapeDtypeStruct((frames, channels), bf16),
        compiler_params=params(1),
        cost_estimate=cost(2 * frames * 256 * channels, 4 * frames * channels),
        name="from_time",
    )(place, *pieces)


def turn_body(sizes, rows, place_ref, *refs):
    pieces, out = refs[:-1], refs[-1]
    count, width = len(pieces), pieces[0].shape[2]
    nz, ny, nx = sizes
    for r, piece in enumerate(pieces):
        shard = (place_ref[3] + count - r) % count
        for tile in range(width // GROUP):
            block = piece[:, :, tile * GROUP : (tile + 1) * GROUP]
            turned = block.reshape(-1, GROUP).T
            for j in range(GROUP // rows):
                owner = shard * (width // rows) + tile * (GROUP // rows) + j
                oz, oy, ox = coordinates(owner, sizes)
                dz = (oz - place_ref[0] + nz) % nz
                dy = (oy - place_ref[1] + ny) % ny
                dx = (ox - place_ref[2] + nx) % nx
                out[pl.ds((dx * ny + dy) * nz + dz, 1)] = turned[j * rows : (j + 1) * rows][None]


def turn(place, pieces, sizes):
    horizon, samples, width = pieces[0].shape
    count = sizes[0] * sizes[1] * sizes[2]
    channels = width * len(pieces)
    rows = channels // count
    frames = horizon * samples
    return pl.pallas_call(
        functools.partial(turn_body, sizes, rows),
        in_specs=[pl.BlockSpec(memory_space=pltpu.SMEM)]
        + [pl.BlockSpec(memory_space=pltpu.VMEM)] * len(pieces),
        out_specs=pl.BlockSpec(memory_space=pltpu.VMEM),
        out_shape=jax.ShapeDtypeStruct((count, rows, frames), bf16),
        compiler_params=pltpu.CompilerParams(vmem_limit_bytes=VMEM_LIMIT),
        cost_estimate=cost(0, 4 * frames * channels),
        name="turn",
    )(place, *pieces)


def zero_ends(padded):
    steps = padded.shape[0]
    zeros = jnp.zeros((HALF,) + padded.shape[1:], padded.dtype)
    padded[:HALF] = zeros
    padded[steps - HALF :] = zeros


def block_copies(sizes, ordered, place_ref, pieces, target, sems, base):
    nz, ny, nx = sizes
    rows = pieces[0].shape[-2]
    copies = []
    for dx in range(nx):
        for dy in range(ny):
            for r in range(nz):
                z = r if ordered else (place_ref[0] - r + nz) % nz
                owner = flat((z, (place_ref[1] - dy + ny) % ny, (place_ref[2] - dx + nx) % nx), sizes)
                at = pl.ds(pl.multiple_of(owner * target[1] + target[2], BLOCK), rows)
                copies.append(
                    pltpu.make_async_copy(
                        pieces[dx * ny + dy].at[r],
                        target[0].at[..., at, :],
                        sems.at[base + len(copies)],
                    )
                )
    return copies


def weight_copies(sizes, cut, place_ref, firsts, seconds, weight, sems):
    rows = firsts[0].shape[2]
    copies = block_copies(
        sizes, True, place_ref, firsts, (weight.at[pl.ds(0, cut)], rows, 0), sems, 0
    )
    return copies + block_copies(
        sizes,
        True,
        place_ref,
        seconds,
        (weight.at[pl.ds(cut, KERNEL - cut)], rows, 0),
        sems,
        len(copies),
    )


def column_copies(place_ref, pieces, target, sems, first_sem):
    count, width = len(pieces), pieces[0].shape[-1]
    copies = []
    for r, piece in enumerate(pieces):
        column = pl.multiple_of(((place_ref[3] + count - r) % count) * width, width)
        copies.append(
            pltpu.make_async_copy(
                piece, target.at[..., pl.ds(column, width)], sems.at[first_sem + r]
            )
        )
    return copies


def group_mean(value):
    return jnp.sum(jnp.sum(value, axis=0), axis=1, keepdims=True)[None] / (HORIZON * GROUP)


def norm_of(a):
    centre = a - group_mean(a)
    spread = lax.rsqrt(group_mean(centre * centre) + EPSILON)
    return centre * spread, spread


def norm_back(h, unit, spread):
    return spread * (h - group_mean(h) - unit * group_mean(h * unit))


def conv_blocks(padded, weight_of, order, body):
    samples, channels = padded.shape[1:]
    for b in range(samples // BLOCK):
        at = slice(b * BLOCK, (b + 1) * BLOCK)
        total = None
        for k in range(KERNEL):
            start = order(k)
            rows = padded[start : start + HORIZON, at, :].reshape(HORIZON * BLOCK, channels)
            part = weight_of(rows, k)
            total = part if total is None else total + part
        body(at, total.reshape(HORIZON, BLOCK, total.shape[1]))


def conv_front(sizes, cut, place_ref, inputs, firsts, seconds, quarters, padded, weight, sems):
    n = pl.program_id(0)
    count = len(quarters)
    height = weight.shape[2]
    base = len(firsts) * sizes[0] * 2 + len(inputs)

    def out_copies():
        return [
            pltpu.make_async_copy(
                weight.at[
                    :, pl.ds(pl.multiple_of(((place_ref[3] + r) % count) * height, height), height), :
                ],
                quarter,
                sems.at[base + r],
            )
            for r, quarter in enumerate(quarters)
        ]

    @pl.when(n == 0)
    def _():
        copies = weight_copies(sizes, cut, place_ref, firsts, seconds, weight, sems)
        copies += column_copies(
            place_ref, inputs, padded.at[pl.ds(HALF, HORIZON)], sems, len(copies)
        )
        for copy in copies:
            copy.start()
        zero_ends(padded)
        for copy in copies:
            copy.wait()
        for copy in out_copies():
            copy.start()

    def finish():
        @pl.when(n == pl.num_programs(0) - 1)
        def _():
            for copy in out_copies():
                copy.wait()

    return finish


def conv_weight(weight, tile):
    column = pl.ds(pl.multiple_of(pl.program_id(0) * tile, tile), tile)

    def apply(rows, k):
        return jnp.dot(rows, weight[k, :, column], preferred_element_type=f32)

    return apply


def groups_of(width):
    return [(g, slice(g * GROUP, (g + 1) * GROUP)) for g in range(width // GROUP)]


def first_body(sizes, cut, shards, place_ref, *refs):
    count = sizes[1] * sizes[2]
    inputs, firsts, seconds = refs[:1], refs[1 : 1 + count], refs[1 + count : 1 + 2 * count]
    scale, shifting, gain, shift = refs[1 + 2 * count : 5 + 2 * count]
    unit_out, spread_out, lifted_out = refs[5 + 2 * count : 8 + 2 * count]
    quarters = refs[8 + 2 * count : 8 + 2 * count + shards]
    padded, weight, sems = refs[8 + 2 * count + shards :]
    tile = unit_out.shape[2]
    finish = conv_front(
        sizes, cut, place_ref, inputs, firsts, seconds, quarters, padded, weight, sems
    )

    def body(at, a):
        for group, lanes in groups_of(tile):
            unit, spread = norm_of(a[:, :, lanes])
            unit_out[:, at, lanes] = unit
            spread_out[group, at, :] = jnp.broadcast_to(spread[0], (BLOCK, GROUP))
            mixed = mish_act(unit * gain[:, lanes][None] + shift[:, lanes][None])
            lifted = scale[at, lanes][None] * mixed + shifting[at, lanes][None]
            lifted_out[:, at, lanes] = lifted.astype(bf16)

    conv_blocks(padded, conv_weight(weight, tile), lambda k: k, body)
    finish()


def second_body(sizes, cut, shards, place_ref, *refs):
    count = sizes[1] * sizes[2]
    inputs, refs = refs[:shards], refs[shards:]
    firsts, seconds = refs[:count], refs[count : 2 * count]
    features, upstream, gain, shift = refs[2 * count : 4 + 2 * count]
    block_out, grad_out, sums_out = refs[4 + 2 * count : 7 + 2 * count]
    quarters = refs[7 + 2 * count : 7 + 2 * count + shards]
    padded, weight, sems = refs[7 + 2 * count + shards :]
    tile = block_out.shape[2]
    finish = conv_front(
        sizes, cut, place_ref, inputs, firsts, seconds, quarters, padded, weight, sems
    )
    sums_out[...] = jnp.zeros_like(sums_out)

    def body(at, a):
        for _, lanes in groups_of(tile):
            unit, spread = norm_of(a[:, :, lanes])
            gain_here = gain[:, lanes][None]
            normed = unit * gain_here + shift[:, lanes][None]
            w, r, t = mish_parts(normed)
            block = features[:, at, lanes].astype(f32) + normed * t
            block_out[:, at, lanes] = block.astype(bf16)
            slope = t + normed * (4.0 * w * (1.0 + w)) * (r * r)
            grad = upstream[:, at, lanes].astype(f32) * slope
            sums_out[0:1, lanes] += jnp.sum(jnp.sum(grad * unit, axis=0), axis=0, keepdims=True)
            sums_out[1:2, lanes] += jnp.sum(jnp.sum(grad, axis=0), axis=0, keepdims=True)
            grad_out[:, at, lanes] = norm_back(grad * gain_here, unit, spread).astype(bf16)

    conv_blocks(padded, conv_weight(weight, tile), lambda k: k, body)
    finish()


def conv_call(body, name, place, sizes, cut, inputs, pieces, extras, extra_specs, outs, out_specs):
    shards = lax.axis_size("shard")
    horizon, samples, _ = inputs[0].shape
    channels = inputs[0].shape[2] * len(inputs)
    frames = horizon * samples
    firsts, seconds = pieces
    width = firsts[0].shape[3]
    tile = min(256, width)
    quarter = jax.ShapeDtypeStruct((KERNEL, width, width), bf16)
    anywhere = pl.BlockSpec(memory_space=pl.ANY)
    copies = 2 * len(firsts) * sizes[0] + len(inputs) + shards
    return pl.pallas_call(
        functools.partial(body, sizes, cut, shards),
        grid_spec=pltpu.PrefetchScalarGridSpec(
            num_scalar_prefetch=1,
            grid=(width // tile,),
            in_specs=[anywhere] * (len(inputs) + 2 * len(firsts)) + extra_specs,
            out_specs=out_specs + [anywhere] * shards,
            scratch_shapes=[
                pltpu.VMEM((HORIZON + 2 * HALF, samples, channels), bf16),
                pltpu.VMEM((KERNEL, channels, width), bf16),
                pltpu.SemaphoreType.DMA((copies,)),
            ],
        ),
        out_shape=outs + [quarter] * shards,
        compiler_params=params(1),
        cost_estimate=cost(
            2 * KERNEL * frames * channels * width, 24 * frames * width + 10 * channels * width
        ),
        name=name,
    )(place, *inputs, *firsts, *seconds, *extras)


def back_front(place_ref, grads, quarters, padded, weight, sems):
    @pl.when(pl.program_id(0) == 0)
    def _():
        copies = column_copies(place_ref, grads, padded.at[pl.ds(HALF, HORIZON)], sems, 0)
        copies += column_copies(place_ref, quarters, weight, sems, len(copies))
        for copy in copies:
            copy.start()
        zero_ends(padded)
        for copy in copies:
            copy.wait()


def back_weight(weight, tile):
    at = pl.ds(pl.multiple_of(pl.program_id(0) * tile, tile), tile)

    def apply(rows, k):
        return lax.dot_general(
            rows, weight[k, at, :], (((1,), (1,)), ((), ())), preferred_element_type=f32
        )

    return apply


def lifted_back_body(shards, place_ref, *refs):
    grads, quarters, refs = refs[:shards], refs[shards : 2 * shards], refs[2 * shards :]
    unit_in, spread_in, scale, gain, shift = refs[:5]
    grad_out, film_out, sums_out = refs[5:8]
    padded, weight, sems = refs[8:]
    tile = grad_out.shape[2]
    back_front(place_ref, grads, quarters, padded, weight, sems)
    sums_out[...] = jnp.zeros_like(sums_out)

    def body(at, a):
        for group, lanes in groups_of(tile):
            grad_lifted = a[:, :, lanes]
            unit = unit_in[:, at, lanes]
            spread = spread_in[group, at, :][None]
            gain_here = gain[:, lanes][None]
            normed = unit * gain_here + shift[:, lanes][None]
            w, r, t = mish_parts(normed)
            film_out[0, at, lanes] = jnp.sum(grad_lifted * (normed * t), axis=0)
            film_out[1, at, lanes] = jnp.sum(grad_lifted, axis=0)
            slope = t + normed * (4.0 * w * (1.0 + w)) * (r * r)
            grad = grad_lifted * scale[at, lanes][None] * slope
            sums_out[0:1, lanes] += jnp.sum(jnp.sum(grad * unit, axis=0), axis=0, keepdims=True)
            sums_out[1:2, lanes] += jnp.sum(jnp.sum(grad, axis=0), axis=0, keepdims=True)
            grad_out[:, at, lanes] = norm_back(grad * gain_here, unit, spread).astype(bf16)

    conv_blocks(padded, back_weight(weight, tile), lambda k: KERNEL - 1 - k, body)


def features_back_body(shards, place_ref, *refs):
    grads, quarters, refs = refs[:shards], refs[shards : 2 * shards], refs[2 * shards :]
    upstream, grad_out, padded, weight, sems = refs
    tile = grad_out.shape[2]
    back_front(place_ref, grads, quarters, padded, weight, sems)

    def body(at, a):
        grad_out[:, at, :] = (a + upstream[:, at, :].astype(f32)).astype(bf16)

    conv_blocks(padded, back_weight(weight, tile), lambda k: KERNEL - 1 - k, body)


def back_call(body, name, place, grads, quarters, extras, extra_specs, outs, out_specs):
    shards = len(grads)
    horizon, samples, width = grads[0].shape
    channels = width * shards
    frames = horizon * samples
    tile = min(256, width)
    anywhere = pl.BlockSpec(memory_space=pl.ANY)
    return pl.pallas_call(
        functools.partial(body, shards),
        grid_spec=pltpu.PrefetchScalarGridSpec(
            num_scalar_prefetch=1,
            grid=(width // tile,),
            in_specs=[anywhere] * (2 * shards) + extra_specs,
            out_specs=out_specs,
            scratch_shapes=[
                pltpu.VMEM((HORIZON + 2 * HALF, samples, channels), bf16),
                pltpu.VMEM((KERNEL, width, channels), bf16),
                pltpu.SemaphoreType.DMA((2 * shards,)),
            ],
        ),
        out_shape=outs,
        compiler_params=params(1),
        cost_estimate=cost(
            2 * KERNEL * frames * channels * width, 24 * frames * width + 10 * channels * width
        ),
        name=name,
    )(place, *grads, *quarters, *extras)


def weight_grad_body(sizes, start, taps, order, half, place_ref, turned, grads, *refs):
    nz = sizes[0]
    near, far = order
    if half is None:
        keep, send, padded = refs
    else:
        embedded, low, keep, send, padded = refs
    rows, frames = turned.shape[2:]
    width = grads.shape[2]
    step = pl.program_id(0)
    away = step // sizes[far] + 1
    across = step % sizes[far]
    stays = away == sizes[near]

    @pl.when(step == 0)
    def _():
        zero_ends(padded)
        padded[HALF : HALF + HORIZON] = grads[...]

    lhs = turned[0].reshape(nz * rows, frames)
    parts = []
    for k in range(start, start + taps):
        at = KERNEL - 1 - k
        rhs = padded[at : at + HORIZON].reshape(frames, width)
        part = jnp.dot(lhs, rhs, preferred_element_type=f32)
        parts.append((k - start, part.reshape(nz, rows, width)))

    extra = []
    if half is not None:
        depth = embedded.shape[0] // (sizes[0] * sizes[1] * sizes[2])
        offset = [0, 0, 0]
        offset[near] = away % sizes[near]
        offset[far] = across
        for r in range(nz):
            there = [(place_ref[axis] + offset[axis]) % sizes[axis] for axis in range(3)]
            there[0] = (place_ref[0] + r) % nz
            at = pl.ds(pl.multiple_of(flat(there, sizes) * depth, BLOCK), depth)
            extra.append(jnp.dot(embedded[at, :], low[...], preferred_element_type=f32))

    def store(out, dtype):
        for k, part in parts:
            out[:, k * rows : (k + 1) * rows, :] = part.astype(dtype)
        for r, part in enumerate(extra):
            out[r, taps * rows :, :] = part.astype(dtype)

    @pl.when(stays)
    def _():
        store(keep.at[0], f32)

    @pl.when(jnp.logical_not(stays))
    def _():
        store(send.at[0, 0], bf16)


def weight_grad(place, turned, grads, sizes, start, taps, order, film=None):
    nz, ny, nx = sizes
    near, far = order
    _, rows, frames = turned.shape
    horizon, samples, width = grads.shape
    height = taps * rows
    turned = turned.reshape(nx * ny, nz, rows, frames)
    extras, specs, half = [], [], None
    if film is not None:
        embedded, low, half = film
        height += embedded.shape[0] // (nx * ny * nz)
        extras = [embedded, low]
        specs = [
            pl.BlockSpec(embedded.shape, lambda s, _: (0, 0)),
            pl.BlockSpec((samples, width), lambda s, _: (0, half)),
        ]

    def source(s, _):
        away, across = (s // sizes[far] + 1) % sizes[near], s % sizes[far]
        dx, dy = (across, away) if near == 1 else (away, across)
        return (dx * ny + dy, 0, 0, 0)

    leaving = (sizes[near] - 1) * sizes[far]

    def kept(s, _):
        return (jnp.maximum(s - leaving, 0), 0, 0, 0)

    def sent(s, _):
        last = jnp.minimum(s, leaving - 1)
        return (last // sizes[far], last % sizes[far], 0, 0, 0)

    return pl.pallas_call(
        functools.partial(weight_grad_body, sizes, start, taps, order, half),
        grid_spec=pltpu.PrefetchScalarGridSpec(
            num_scalar_prefetch=1,
            grid=(nx * ny,),
            in_specs=[
                pl.BlockSpec((1, nz, rows, frames), source),
                pl.BlockSpec(grads.shape, lambda s, _: (0, 0, 0)),
            ]
            + specs,
            out_specs=[
                pl.BlockSpec((1, nz, height, width), kept),
                pl.BlockSpec((1, 1, nz, height, width), sent),
            ],
            scratch_shapes=[pltpu.VMEM((HORIZON + 2 * HALF, samples, width), bf16)],
        ),
        out_shape=[
            jax.ShapeDtypeStruct((sizes[far], nz, height, width), f32),
            jax.ShapeDtypeStruct((sizes[near] - 1, sizes[far], nz, height, width), bf16),
        ],
        compiler_params=params(1),
        cost_estimate=cost(
            2 * taps * nx * ny * nz * rows * frames * width,
            2 * nx * ny * nz * rows * frames + 6 * taps * nx * ny * nz * rows * width,
        ),
        name="weight_grad",
    )(place, turned, grads, *extras)


def conv_weight_grad(place, turned, grads, sizes, cut, film=None):
    halves = (None, None) if film is None else (film + (0,), film + (1,))
    keep, send = weight_grad(place, turned, grads, sizes, 0, cut, (1, 2), halves[0])
    first = scatter_planes(keep, send, sizes, (1, 2))
    keep, send = weight_grad(place, turned, grads, sizes, cut, KERNEL - cut, (2, 1), halves[1])
    second = scatter_planes(keep, send, sizes, (2, 1))
    return scatter_lines(first, second, sizes)


def film_body(sizes, rows, place_ref, embedded, *refs):
    count = sizes[1] * sizes[2]
    firsts, seconds = refs[:count], refs[count : 2 * count]
    out, weight_out, weight, sems = refs[2 * count :]
    samples = embedded.shape[0]
    cut = firsts[0].shape[1]
    depth = cut + seconds[0].shape[1]
    copies = block_copies(sizes, False, place_ref, firsts, (weight, depth, 0), sems, 0)
    copies += block_copies(
        sizes, False, place_ref, seconds, (weight, depth, cut), sems, len(copies)
    )
    for copy in copies:
        copy.start()
    for copy in copies:
        copy.wait()
    back = pltpu.make_async_copy(weight, weight_out, sems.at[len(copies)])
    back.start()
    out[:samples, :] = jnp.dot(embedded[...], weight[...], preferred_element_type=f32)
    edge = rows // BLOCK * BLOCK
    for d in range(sizes[0] * count):
        block = weight[d * depth + edge : d * depth + edge + BLOCK, :].astype(f32)
        out[samples + d : samples + d + 1, :] = block[rows - edge : rows - edge + 1, :]
    back.wait()


def film_call(place, embedded, pieces, sizes, rows):
    firsts, seconds = pieces
    samples, deep = embedded.shape
    width = firsts[0].shape[2]
    count = sizes[0] * sizes[1] * sizes[2]
    anywhere = pl.BlockSpec(memory_space=pl.ANY)
    whole = pl.BlockSpec(memory_space=pltpu.VMEM)
    return pl.pallas_call(
        functools.partial(film_body, sizes, rows),
        in_specs=[pl.BlockSpec(memory_space=pltpu.SMEM), whole] + [anywhere] * (2 * len(firsts)),
        out_specs=[whole, anywhere],
        out_shape=[
            jax.ShapeDtypeStruct((samples + count, width), f32),
            jax.ShapeDtypeStruct((deep, width), bf16),
        ],
        scratch_shapes=[
            pltpu.VMEM((deep, width), bf16),
            pltpu.SemaphoreType.DMA((2 * count + 1,)),
        ],
        compiler_params=pltpu.CompilerParams(vmem_limit_bytes=VMEM_LIMIT),
        cost_estimate=cost(2 * samples * deep * width, 4 * deep * width),
        name="film",
    )(place, embedded, *firsts, *seconds)


def table_body(low, weight, cond_in, onehot, out):
    grad = lax.dot_general(
        low[...], weight[...], (((1,), (1,)), ((), ())), preferred_element_type=f32
    )
    rest = grad * mish_slope(cond_in[...])
    total = jnp.zeros(out.shape, f32)
    for _ in range(3):
        part = rest.astype(bf16)
        rest = rest - part.astype(f32)
        total = total + jnp.dot(onehot[...], part, preferred_element_type=f32)
    out[...] = total


def table_call(low, weight, cond_in, onehot):
    return pl.pallas_call(
        table_body,
        in_specs=[pl.BlockSpec(memory_space=pltpu.VMEM)] * 4,
        out_specs=pl.BlockSpec(memory_space=pltpu.VMEM),
        out_shape=jax.ShapeDtypeStruct((onehot.shape[0], weight.shape[0]), f32),
        compiler_params=pltpu.CompilerParams(vmem_limit_bytes=VMEM_LIMIT),
        cost_estimate=cost(2 * low.size * weight.shape[0], 2 * weight.size),
        name="table_grad",
    )(low, weight, cond_in, onehot)


def local(
    features,
    condition,
    task_ids,
    conv_first,
    conv_second,
    film_weight,
    norm_gain_first,
    norm_shift_first,
    norm_gain_second,
    norm_shift_second,
    film_bias,
    task_table,
    out_grad,
    grad_mask,
):
    count, shards = lax.axis_size("dp"), lax.axis_size("shard")
    sizes = digits(count)
    nz, ny, nx = sizes
    me, own = lax.axis_index("dp"), lax.axis_index("shard")
    position = coordinates(me, sizes)
    place = jnp.stack([position[0], position[1], position[2], own]).astype(jnp.int32)
    samples = condition.shape[0]
    channels = features.shape[1]
    width = channels // shards
    tile = min(256, width)
    film_rows, film_width = film_weight.shape

    def own_columns(value, each):
        return lax.dynamic_slice_in_dim(value, own * each, each, value.ndim - 1)

    each = norm_gain_first.shape[0]
    tasks = task_table.shape[0]
    depth = -(-(film_rows + 1) // BLOCK) * BLOCK
    film_cut = depth // (2 * BLOCK) * BLOCK

    def deep(value):
        blocks = value.reshape(-1, count, film_rows)
        return jnp.pad(blocks, ((0, 0), (0, 0), (0, depth - film_rows))).reshape(-1, count * depth)

    vectors = jnp.concatenate(
        [norm_gain_first, norm_shift_first, norm_gain_second, norm_shift_second, film_bias]
    )
    vectors = jnp.pad(vectors, (0, film_width - vectors.shape[0]))
    film_block = jnp.concatenate(
        [
            film_weight,
            vectors[None],
            jnp.zeros((depth - film_rows - 1, film_width), bf16),
        ]
    )
    film_pieces = gather_planes(*move_lines(film_block, film_cut, sizes), sizes)
    lines_a = gather_lines(conv_first, HALF + 1, sizes)
    lines_b = gather_lines(conv_second, HALF + 1, sizes)
    onehot = (task_ids[:, None] == jnp.arange(tasks)[None, :]).astype(bf16)
    cond_in = condition.astype(f32) + jnp.dot(onehot, task_table, preferred_element_type=f32)
    cond_in = deep(cond_in)
    embedded = mish_act(cond_in).astype(bf16)
    film_own, film_all = film_call(place, embedded, film_pieces, sizes, film_rows)
    film_out = in_order(around(film_own))
    small = film_out[:, samples:]
    small = jnp.moveaxis(small, 0, 1).reshape(count * shards, film_width)
    gain_a, shift_a, gain_b, shift_b = [
        own_columns(small[:, i * each : (i + 1) * each].reshape(1, -1), width) for i in range(4)
    ]
    bias = small[:, 4 * each : 6 * each].reshape(1, -1)
    film_out = jnp.moveaxis(film_out[:, :samples], 0, 1).reshape(samples, 2 * channels) + bias
    scale = own_columns(film_out[:, :channels], width)
    shifting = own_columns(film_out[:, channels:], width)

    timed, upstream = to_time(features, out_grad, grad_mask)
    turned_a = turn(place, [timed], sizes)
    upstream = own_columns(upstream, width)
    residual = own_columns(timed, width)
    cut_a = cut_b = HALF + 1
    pieces_a = gather_planes(*lines_a, sizes)
    pieces_b = gather_planes(*lines_b, sizes)

    column = pl.BlockSpec((samples, tile), lambda n, _: (0, n))
    vector = pl.BlockSpec((1, tile), lambda n, _: (0, n))
    pair = pl.BlockSpec((2, tile), lambda n, _: (0, n))
    field = pl.BlockSpec((HORIZON, samples, tile), lambda n, _: (0, 0, n))
    spreads = pl.BlockSpec((tile // GROUP, samples, GROUP), lambda n, _: (n, 0, 0))
    films = pl.BlockSpec((2, samples, tile), lambda n, _: (0, 0, n))
    field_shape = (HORIZON, samples, width)
    pair_shape = jax.ShapeDtypeStruct((2, width), f32)
    spread_shape = jax.ShapeDtypeStruct((width // GROUP, samples, GROUP), f32)

    unit_a, spread_a, lifted, *quarters_a = conv_call(
        first_body,
        "conv_first",
        place,
        sizes,
        cut_a,
        [timed],
        pieces_a,
        [scale, shifting, gain_a, shift_a],
        [column, column, vector, vector],
        [jax.ShapeDtypeStruct(field_shape, f32), spread_shape, jax.ShapeDtypeStruct(field_shape, bf16)],
        [field, spreads, field],
    )
    lifted_all = around(lifted)
    turned_b = turn(place, lifted_all, sizes)
    block_own, grad_second, sums_b, *quarters_b = conv_call(
        second_body,
        "conv_second",
        place,
        sizes,
        cut_b,
        lifted_all,
        pieces_b,
        [residual, upstream, gain_b, shift_b],
        [field, field, vector, vector],
        [jax.ShapeDtypeStruct(field_shape, bf16), jax.ShapeDtypeStruct(field_shape, bf16), pair_shape],
        [field, field, pair],
    )
    quarters_a = [quarters_a[0]] + [swap(quarters_a[r], r) for r in range(1, shards)]
    quarters_b = [quarters_b[0]] + [swap(quarters_b[r], r) for r in range(1, shards)]
    block_out = from_time(place, around(block_own))

    rows_b = conv_weight_grad(place, turned_b, grad_second, sizes, cut_b)
    grad_conv_second = rows_b.reshape(conv_second.shape)
    grad_first, grad_film, sums_a = back_call(
        lifted_back_body,
        "lifted_back",
        place,
        around(grad_second),
        quarters_b,
        [unit_a, spread_a, scale, gain_a, shift_a],
        [field, spreads, column, vector, vector],
        [
            jax.ShapeDtypeStruct(field_shape, bf16),
            jax.ShapeDtypeStruct((2, samples, width), f32),
            pair_shape,
        ],
        [field, films, pair],
    )
    low = in_order(around(grad_film.astype(bf16)))
    low = jnp.moveaxis(low, 0, 2).reshape(2, samples, channels)
    low_own = own_columns(jnp.moveaxis(low, 0, 1).reshape(samples, 2 * channels), film_width)
    rows_a = conv_weight_grad(
        place, turned_a, grad_first, sizes, cut_a, (embedded.T, low_own)
    )
    block_rows = conv_first.shape[1]
    ends = [cut_a * block_rows, cut_a * block_rows + depth, KERNEL * block_rows + depth]
    grad_conv_first = jnp.concatenate([rows_a[: ends[0]], rows_a[ends[1] : ends[2]]])
    grad_conv_first = grad_conv_first.reshape(conv_first.shape)
    grad_film_weight = jnp.concatenate(
        [rows_a[ends[0] : ends[0] + film_rows], rows_a[ends[2] : ends[2] + film_rows]], axis=1
    )
    grad_features_own = back_call(
        features_back_body,
        "features_back",
        place,
        around(grad_first),
        quarters_a,
        [upstream],
        [field],
        jax.ShapeDtypeStruct(field_shape, bf16),
        field,
    )
    grad_features = from_time(place, around(grad_features_own))

    task_rows = -(-tasks // BLOCK) * BLOCK
    onehot = jnp.pad(onehot.T, ((0, task_rows - tasks), (0, 0)))
    grad_table = table_call(low_own, film_all, cond_in, onehot)[:tasks]
    sums = jnp.concatenate([sums_a, sums_b, jnp.sum(grad_film, axis=1)])
    sums = lax.dynamic_update_slice(jnp.zeros((6, channels), f32), sums, (0, own * width)).reshape(-1)
    wide = grad_table.shape[1]
    rows = -(-(tasks + -(-sums.shape[0] // wide)) // 8) * 8
    sums = jnp.pad(sums, (0, (rows - tasks) * wide - sums.shape[0])).reshape(rows - tasks, wide)
    total = sum_everywhere(jnp.concatenate([grad_table, sums]), sizes)
    grad_table = total[:tasks].reshape(tasks, count, depth)[:, :, :film_rows].reshape(tasks, -1)
    sums = total[tasks:].reshape(-1)[: 6 * channels].reshape(6, channels)
    index = me * shards + own
    small = [lax.dynamic_slice(sums[i], (index * each,), (each,)) for i in range(4)]
    grad_film_bias = lax.dynamic_slice(sums[4:].reshape(-1), (index * 2 * each,), (2 * each,))
    return (
        block_out,
        grad_features,
        grad_conv_first,
        grad_conv_second,
        grad_film_weight,
        small[0],
        small[1],
        small[2],
        small[3],
        grad_film_bias,
        grad_table,
    )


def solution(mesh):
    return jax.shard_map(
        local,
        mesh=mesh,
        in_specs=(
            P("dp", None),
            P("dp", None),
            P("dp"),
            P(None, "dp", "shard"),
            P(None, "dp", "shard"),
            P("dp", "shard"),
            P(("dp", "shard")),
            P(("dp", "shard")),
            P(("dp", "shard")),
            P(("dp", "shard")),
            P(("dp", "shard")),
            P(),
            P("dp", None),
            P("dp"),
        ),
        out_specs=(
            P("dp", None),
            P("dp", None),
            P(None, "dp", "shard"),
            P(None, "dp", "shard"),
            P("dp", "shard"),
            P(("dp", "shard")),
            P(("dp", "shard")),
            P(("dp", "shard")),
            P(("dp", "shard")),
            P(("dp", "shard")),
            P(),
        ),
        check_vma=False,
    )
```

time: 687 us -> 506 us (0.74); the launches traced: 684 us -> 496 us
  waiting for transfers between devices: 313 us -> 224 us
  blocking collectives: 49.7 us -> 0 us
  local copies, waits for them, and re-layouts: 65.8 us -> 42.8 us
  starting transfers between devices: 58.7 us -> 46.7 us
  Pallas kernels: 147 us -> 137 us
  matrix products: 7.3 us -> 0.26 us
    psum x1 -> x0, waiting for transfers between devices: 119 us -> none  [local(): total = lax.psum(total, ('dp', 'shard'))]
    all_gather x1 -> x0, blocking collectives: 49.7 us -> none  [local(): lax.all_gather(block, ('dp', 'shard'), axis=0, tiled=False).astype(f32)]
    ppermute x48 -> x35, waiting for transfers between devices: 193 us -> 213 us  [move(): return lax.ppermute(value, 'dp', pairs)]
    ppermute x48 -> x35, starting transfers between devices: 57.8 us -> 40 us  [move(): return lax.ppermute(value, 'dp', pairs)]
    pallas_call x2, Pallas kernels: 53.7 us -> 37.9 us  [conv_call(): pl.pallas_call(functools.partial(body, sizes, cut, shards), grid_spec=plt...]
    gather x7 -> x0, local copies, waits for them, and re-layouts: 13.5 us -> none  [the longest x5 8.58 us: ordered(): value.reshape(-1, count, film_rows)[:, order].reshape(-1, count * film_rows)]
    pallas_call x4 -> x6, Pallas kernels: 28.8 us -> 42.2 us  [the longest x4 35.5 us: weight_grad(): pl.pallas_call(functools.partial(weight_grad_body, sizes, start, taps, or...]
    ppermute x0 -> x4, waiting for transfers between devices: none -> 9.81 us  [trade(): return lax.ppermute(value, 'dp', pairs)]
  transfers between devices with their start and end apart: 58 -> 52, of which waited for: 24 -> 27; matrix products, arithmetic and copies ran while one was open for 13% -> 10% of each run, Pallas kernels for 15% -> 23%
where the time goes in v2:
time: 506 us; the launch traced here: 496 us
  waiting for transfers between devices  224 us (44%)
  Pallas kernels  137 us (27%)
  starting transfers between devices  46.7 us (9%)
  local copies, waits for them, and re-layouts  42.8 us (8%)
  other arithmetic  29.2 us (6%)
  between operations  15.5 us (3%)
    ppermute x35, waiting for transfers between devices, move(): return lax.ppermute(value, 'dp', pairs)  213 us
    ppermute x35, starting transfers between devices, move(): return lax.ppermute(value, 'dp', pairs)  40 us
    pallas_call x2, Pallas kernels, conv_call(): pl.pallas_call(functools.partial(body, sizes, cut, shards), grid_spec=plt...  37.9 us
    pallas_call x4, Pallas kernels, weight_grad(): pl.pallas_call(functools.partial(weight_grad_body, sizes, start, taps, or...  35.5 us
    pallas_call x2, Pallas kernels, back_call(): pl.pallas_call(functools.partial(body, shards), grid_spec=pltpu.PrefetchS...  32.6 us
    unnamed x82, local copies, waits for them, and re-layouts  15.5 us
    pallas_call x2, Pallas kernels, from_time(): pl.pallas_call(from_time_body, grid_spec=pltpu.PrefetchScalarGridSpec(num...  10.7 us
  transfers between devices with their start and end apart: 52, of which 27 were waited for; matrix products, arithmetic and copies ran while one was open for 10% of the time, Pallas kernels for 23%

profile of v2, /device:TPU:10, one launch (start us, length us, event | category | flops | bytes accessed | tf_op | source)
XLA Modules:
  0.0 495.9 jit_solution(15415633287410603343)
XLA Ops:
  18.5 8.4 %collective-permute-done.7 = bf16[80,1024]{1,0:T(8,128)(2,1)S(1)} collective-permute-done((bf16[80,1024]{1,0:T(8,128)(2,1)S(1)}, bf16[80,1024]{1,0:T(8,128)(2,1)S(1)}, u32[]{:S(2)}, u32[]{:S(2)}) %collective-permute-start.7) | collective-permute-done | bytes 163872 | tf_op jit(solution)/shard_map/ppermute | solution.py:60
  26.9 11.6 %collective-permute-done.6 = bf16[80,1024]{1,0:T(8,128)(2,1)S(1)} collective-permute-done((bf16[80,1024]{1,0:T(8,128)(2,1)S(1)}, bf16[80,1024]{1,0:T(8,128)(2,1)S(1)}, u32[]{:S(2)}, u32[]{:S(2)}) %collective-permute-start.6) | collective-permute-done | bytes 163872 | tf_op jit(solution)/shard_map/ppermute | solution.py:60
  44.3 5.4 %collective-permute-done.10.refs_2_ = bf16[4,32,1024]{2,1,0:T(8,128)(2,1)S(1)} collective-permute-done((bf16[4,32,1024]{2,1,0:T(8,128)(2,1)S(1)}, bf16[4,32,1024]{2,1,0:T(8,128)(2,1)S(1)}, u32[]{:S(2)}, u32[]{:S(2)}) %collective-permute-start.10) | collective-permute-done | bytes 262176 | tf_op jit(solution)/shard_map/ppermute | solution.py:60
  60.9 5.3 %film.1 = (f32[112,1024]{1,0:T(8,128)S(1)}, bf16[1280,1024]{1,0:T(8,128)(2,1)S(1)}) custom-call(s32[4]{0:T(128)S(1)} %pad_add_fusion.place_ref, bf16[96,1280]{1,0:T(8,128)(2,1)S(1)} %copy.36.embedded, bf16[4,32,1024]{2,1,0:T(8,128)(2,1)S(1)} %pad_maximum_fusion.10.refs_0_, bf16[4,32,1024]{2,1,0:T(8,128)(2,1)S(1)} %copy-done.14, ...), custom_call_target="tpu_custom_call" | custom-call | flops 251658240 | bytes 5242880 | tf_op jit(solution)/shard_map/film/pallas_call | solution.py:749
  67.9 7.0 %to_time.1 = (bf16[16,96,1024]{2,1,0:T(8,128)(2,1)S(1)}, bf16[16,96,1024]{2,1,0:T(8,128)(2,1)}) custom-call(bf16[1536,1024]{1,0:T(8,128)(2,1)} %features_ref.1, bf16[1536,1024]{1,0:T(8,128)(2,1)} %grads_ref.1, s32[6,1,256]{2,1,0:T(1,128)S(1)} %reshape.119.mask_ref), custom_call_target="tpu_custom_call" | custom-call | flops 1610612736 | bytes 12582912 | tf_op jit(solution)/shard_map/to_time/pallas_call | solution.py:198
  85.0 12.8 %collective-permute-done.1.refs_3_ = bf16[4,3,64,512]{3,2,1,0:T(8,128)(2,1)S(1)} collective-permute-done((bf16[4,3,64,512]{3,2,1,0:T(8,128)(2,1)S(1)}, bf16[4,3,64,512]{3,2,1,0:T(8,128)(2,1)S(1)}, u32[]{:S(2)}, u32[]{:S(2)}) %collective-permute-start.1) | collective-permute-done | bytes 786464 | tf_op jit(solution)/shard_map/ppermute | solution.py:60
  106.8 6.8 %collective-permute-done.4.refs_7_ = bf16[4,2,64,512]{3,2,1,0:T(8,128)(2,1)} collective-permute-done((bf16[4,2,64,512]{3,2,1,0:T(8,128)(2,1)S(1)}, bf16[4,2,64,512]{3,2,1,0:T(8,128)(2,1)}, u32[]{:S(2)}, u32[]{:S(2)}) %collective-permute-start.4) | collective-permute-done | bytes 524320 | tf_op jit(solution)/shard_map/ppermute | solution.py:60
  114.5 10.3 %collective-permute-done.5.refs_8_ = bf16[4,2,64,512]{3,2,1,0:T(8,128)(2,1)} collective-permute-done((bf16[4,2,64,512]{3,2,1,0:T(8,128)(2,1)}, bf16[4,2,64,512]{3,2,1,0:T(8,128)(2,1)}, u32[]{:S(2)}, u32[]{:S(2)}) %collective-permute-start.5) | collective-permute-done | bytes 524320 | tf_op jit(solution)/shard_map/ppermute | solution.py:60
  124.8 5.1 %collective-permute-done.2.refs_4_ = bf16[4,3,64,512]{3,2,1,0:T(8,128)(2,1)} collective-permute-done((bf16[4,3,64,512]{3,2,1,0:T(8,128)(2,1)S(1)}, bf16[4,3,64,512]{3,2,1,0:T(8,128)(2,1)}, u32[]{:S(2)}, u32[]{:S(2)}) %collective-permute-start.2) | collective-permute-done | bytes 786464 | tf_op jit(solution)/shard_map/ppermute | solution.py:60
  136.2 17.3 %conv_first.1 = (f32[16,96,512]{2,1,0:T(8,128)}, f32[4,96,128]{2,1,0:T(8,128)S(1)}, bf16[16,96,512]{2,1,0:T(8,128)(2,1)}, bf16[5,512,512]{2,1,0:T(8,128)(2,1)}, bf16[5,512,512]{2,1,0:T(8,128)(2,1)}) custom-call(s32[4]{0:T(128)S(1)} %pad_add_fusion.place_ref, bf16[16,96,1024]{2,1,0:T(8,128)(2,1)} %copy-done.2, bf16[4,3,64,512]{3,2,1,0:T(8,128)(2,1)S(1)} %copy-done.10, ...), custom_call_target="tpu_custom_call" | custom-call | flops 8053063680 | bytes 24117248 | tf_op jit(solution)/shard_map/conv_first/pallas_call | solution.py:480
  159.5 11.0 %collective-permute-done.20.refs_7_ = bf16[4,2,64,512]{3,2,1,0:T(8,128)(2,1)} collective-permute-done((bf16[4,2,64,512]{3,2,1,0:T(8,128)(2,1)}, bf16[4,2,64,512]{3,2,1,0:T(8,128)(2,1)}, u32[]{:S(2)}, u32[]{:S(2)}) %collective-permute-start.20) | collective-permute-done | bytes 524320 | tf_op jit(solution)/shard_map/ppermute | solution.py:60
  174.2 13.1 %collective-permute-done.17.refs_3_ = bf16[4,3,64,512]{3,2,1,0:T(8,128)(2,1)} collective-permute-done((bf16[4,3,64,512]{3,2,1,0:T(8,128)(2,1)}, bf16[4,3,64,512]{3,2,1,0:T(8,128)(2,1)}, u32[]{:S(2)}, u32[]{:S(2)}) %collective-permute-start.17) | collective-permute-done | bytes 786464 | tf_op jit(solution)/shard_map/ppermute | solution.py:60
  187.3 16.4 %collective-permute-done.19.refs_5_ = bf16[4,3,64,512]{3,2,1,0:T(8,128)(2,1)} collective-permute-done((bf16[4,3,64,512]{3,2,1,0:T(8,128)(2,1)}, bf16[4,3,64,512]{3,2,1,0:T(8,128)(2,1)}, u32[]{:S(2)}, u32[]{:S(2)}) %collective-permute-start.19) | collective-permute-done | bytes 786464 | tf_op jit(solution)/shard_map/ppermute | solution.py:60
  203.8 20.6 %conv_second.1 = (bf16[16,96,512]{2,1,0:T(8,128)(2,1)}, bf16[16,96,512]{2,1,0:T(8,128)(2,1)}, f32[2,512]{1,0:T(2,128)S(1)}, bf16[5,512,512]{2,1,0:T(8,128)(2,1)}, bf16[5,512,512]{2,1,0:T(8,128)(2,1)}) custom-call(s32[4]{0:T(128)S(1)} %pad_add_fusion.place_ref, bf16[16,96,512]{2,1,0:T(8,128)(2,1)} %get-tuple-element.38.refs_0_, ...), custom_call_target="tpu_custom_call" | custom-call | flops 8053063680 | bytes 24117248 | tf_op jit(solution)/shard_map/conv_second/pallas_call | solution.py:480
  228.5 6.6 %weight_grad.7 = (f32[2,4,128,512]{3,2,1,0:T(8,128)S(1)}, bf16[1,2,4,128,512]{4,3,2,1,0:T(8,128)(2,1)S(1)}) custom-call(s32[4]{0:T(128)S(1)} %pad_add_fusion.place_ref, bf16[4,4,64,1536]{3,2,1,0:T(8,128)(2,1)} %bitcast.131, bf16[16,96,512]{2,1,0:T(8,128)(2,1)} %get-tuple-element.41.refs_0_.grads), custom_call_target="tpu_custom_call" | custom-call | flops 3221225472 | bytes 9437184 | tf_op jit(solution)/shard_map/weight_grad/pallas_call | solution.py:679
  236.7 9.8 %weight_grad.6 = (f32[2,4,192,512]{3,2,1,0:T(8,128)}, bf16[1,2,4,192,512]{4,3,2,1,0:T(8,128)(2,1)}) custom-call(s32[4]{0:T(128)S(1)} %pad_add_fusion.place_ref, bf16[4,4,64,1536]{3,2,1,0:T(8,128)(2,1)} %bitcast.132, bf16[16,96,512]{2,1,0:T(8,128)(2,1)} %get-tuple-element.41.refs_0_.grads), custom_call_target="tpu_custom_call" | custom-call | flops 4831838208 | bytes 12582912 | tf_op jit(solution)/shard_map/weight_grad/pallas_call | solution.py:679
  247.0 13.7 %collective-permute-done.39 = bf16[2,4,128,512]{3,2,1,0:T(8,128)(2,1)S(1)} collective-permute-done((bf16[2,4,128,512]{3,2,1,0:T(8,128)(2,1)S(1)}, bf16[2,4,128,512]{3,2,1,0:T(8,128)(2,1)S(1)}, u32[]{:S(2)}, u32[]{:S(2)}) %collective-permute-start.39) | collective-permute-done | bytes 1048608 | tf_op jit(solution)/shard_map/ppermute | solution.py:60
  270.1 13.9 %collective-permute-done.37 = bf16[2,4,192,512]{3,2,1,0:T(8,128)(2,1)} collective-permute-done((bf16[2,4,192,512]{3,2,1,0:T(8,128)(2,1)}, bf16[2,4,192,512]{3,2,1,0:T(8,128)(2,1)}, u32[]{:S(2)}, u32[]{:S(2)}) %collective-permute-start.37) | collective-permute-done | bytes 1572896 | tf_op jit(solution)/shard_map/ppermute | solution.py:60
  287.5 7.0 %collective-permute-done.40 = bf16[4,128,512]{2,1,0:T(8,128)(2,1)} collective-permute-done((bf16[4,128,512]{2,1,0:T(8,128)(2,1)S(1)}, bf16[4,128,512]{2,1,0:T(8,128)(2,1)}, u32[]{:S(2)}, u32[]{:S(2)}) %collective-permute-start.40) | collective-permute-done | bytes 524320 | tf_op jit(solution)/shard_map/ppermute | solution.py:60
  296.9 18.4 %lifted_back.1 = (bf16[16,96,512]{2,1,0:T(8,128)(2,1)}, f32[2,96,512]{2,1,0:T(8,128)S(1)}, f32[2,512]{1,0:T(2,128)S(1)}) custom-call(s32[4]{0:T(128)S(1)} %pad_add_fusion.place_ref, bf16[16,96,512]{2,1,0:T(8,128)(2,1)} %get-tuple-element.41.refs_0_.grads, bf16[16,96,512]{2,1,0:T(8,128)(2,1)} %collective-permute-done.24.refs_1_, ...), custom_call_target="tpu_custom_call" | custom-call | flops 8053063680 | bytes 24117248 | tf_op jit(solution)/shard_map/lifted_back/pallas_call | solution.py:572
  321.8 15.3 %collective-permute-done.38 = bf16[4,192,512]{2,1,0:T(8,128)(2,1)} collective-permute-done((bf16[4,192,512]{2,1,0:T(8,128)(2,1)}, bf16[4,192,512]{2,1,0:T(8,128)(2,1)}, u32[]{:S(2)}, u32[]{:S(2)}) %collective-permute-start.38) | collective-permute-done | bytes 786464 | tf_op jit(solution)/shard_map/ppermute | solution.py:60
  340.1 5.1 %collective-permute-done.45 = f32[28,1280]{1,0:T(8,128)S(1)} collective-permute-done((f32[28,1280]{1,0:T(8,128)S(1)}, f32[28,1280]{1,0:T(8,128)S(1)}, u32[]{:S(2)}, u32[]{:S(2)}) %collective-permute-start.45) | collective-permute-done | bytes 143392 | tf_op jit(solution)/shard_map/ppermute | solution.py:79
  346.0 4.7 collective-permute-done.46
  350.8 10.1 %weight_grad.4 = (f32[2,4,272,512]{3,2,1,0:T(8,128)}, bf16[1,2,4,272,512]{4,3,2,1,0:T(8,128)(2,1)S(1)}) custom-call(s32[4]{0:T(128)S(1)} %pad_add_fusion.place_ref, bf16[4,4,64,1536]{3,2,1,0:T(8,128)(2,1)} %bitcast.123, bf16[16,96,512]{2,1,0:T(8,128)(2,1)} %get-tuple-element.46.refs_0_.grads, bf16[1280,96]{1,0:T(8,128)(2,1)S(1)} %bitcast.125, ...), custom_call_target="tpu_custom_call" | custom-call | flops 4831838208 | bytes 12582912 | tf_op jit(solution)/shard_map/weight_grad/pallas_call | solution.py:679
  366.7 8.9 %weight_grad.5 = (f32[2,4,208,512]{3,2,1,0:T(8,128)}, bf16[1,2,4,208,512]{4,3,2,1,0:T(8,128)(2,1)}) custom-call(s32[4]{0:T(128)S(1)} %pad_add_fusion.place_ref, bf16[4,4,64,1536]{3,2,1,0:T(8,128)(2,1)} %bitcast.124, bf16[16,96,512]{2,1,0:T(8,128)(2,1)} %get-tuple-element.46.refs_0_.grads, bf16[1280,96]{1,0:T(8,128)(2,1)S(1)} %bitcast.126, ...), custom_call_target="tpu_custom_call" | custom-call | flops 3221225472 | bytes 9437184 | tf_op jit(solution)/shard_map/weight_grad/pallas_call | solution.py:679
  380.1 6.4 %from_time.2 = bf16[1536,1024]{1,0:T(8,128)(2,1)} custom-call(s32[4]{0:T(128)S(1)} %pad_add_fusion.place_ref, bf16[16,96,512]{2,1,0:T(8,128)(2,1)S(1)} %copy-done.7, bf16[16,96,512]{2,1,0:T(8,128)(2,1)} %collective-permute-done.23.refs_1_), custom_call_target="tpu_custom_call" | custom-call | flops 805306368 | bytes 6291456 | tf_op jit(solution)/shard_map/from_time/pallas_call | solution.py:224
  396.9 16.7 %collective-permute-done.32 = bf16[2,4,208,512]{3,2,1,0:T(8,128)(2,1)} collective-permute-done((bf16[2,4,208,512]{3,2,1,0:T(8,128)(2,1)}, bf16[2,4,208,512]{3,2,1,0:T(8,128)(2,1)}, u32[]{:S(2)}, u32[]{:S(2)}) %collective-permute-start.32) | collective-permute-done | bytes 1703968 | tf_op jit(solution)/shard_map/ppermute | solution.py:60
  422.6 14.1 %features_back.1.refs_0_ = bf16[16,96,512]{2,1,0:T(8,128)(2,1)S(1)} custom-call(s32[4]{0:T(128)S(1)} %pad_add_fusion.place_ref, bf16[16,96,512]{2,1,0:T(8,128)(2,1)} %get-tuple-element.46.refs_0_.grads, bf16[16,96,512]{2,1,0:T(8,128)(2,1)} %collective-permute-done.26.refs_1_, bf16[5,512,512]{2,1,0:T(8,128)(2,1)} %get-tuple-element.47.refs_2_, ...), custom_call_target="tpu_custom_call" | custom-call | flops 8053063680 | bytes 24117248 | tf_op jit(solution)/shard_map/features_back/pallas_call | solution.py:572
  438.5 5.7 %collective-permute-done.31 = bf16[4,272,512]{2,1,0:T(8,128)(2,1)} collective-permute-done((bf16[4,272,512]{2,1,0:T(8,128)(2,1)}, bf16[4,272,512]{2,1,0:T(8,128)(2,1)}, u32[]{:S(2)}, u32[]{:S(2)}) %collective-permute-start.31) | collective-permute-done | bytes 1114144 | tf_op jit(solution)/shard_map/ppermute | solution.py:60
  451.7 4.3 from_time.3
  456.1 19.1 %collective-permute-done.35 = bf16[480,512]{1,0:T(8,128)(2,1)S(1)} collective-permute-done((bf16[480,512]{1,0:T(8,128)(2,1)S(1)}, bf16[480,512]{1,0:T(8,128)(2,1)S(1)}, u32[]{:S(2)}, u32[]{:S(2)}) %collective-permute-start.35) | collective-permute-done | bytes 491552 | tf_op jit(solution)/shard_map/ppermute | solution.py:60
  475.2 11.4 %collective-permute-done.36 = bf16[480,512]{1,0:T(8,128)(2,1)S(1)} collective-permute-done((bf16[480,512]{1,0:T(8,128)(2,1)S(1)}, bf16[480,512]{1,0:T(8,128)(2,1)S(1)}, u32[]{:S(2)}, u32[]{:S(2)}) %collective-permute-start.36) | collective-permute-done | bytes 491552 | tf_op jit(solution)/shard_map/ppermute | solution.py:60
  (287 shorter events, 137.8 us)
Async XLA Ops:
  7.2 69.3 %all-gather.5.cloned.1.call-start = ((), (), s32[]{:S(2)}) async-start(), calls=%async_computation | async-start | bytes 1638400 | tf_op jit(solution)/shard_map/all_gather | solution.py:88
  15.0 23.6 %collective-permute-start.6 = (bf16[80,1024]{1,0:T(8,128)(2,1)S(1)}, bf16[80,1024]{1,0:T(8,128)(2,1)S(1)}, u32[]{:S(2)}, u32[]{:S(2)}) collective-permute-start(bf16[80,1024]{1,0:T(8,128)(2,1)S(1)} %maximum_maximum_fusion), channel_id=1, source_target_pairs={{0,8},{2,10},{4,12},{6,14},{8,16},{10,18},{12,20},{14,22},{16,24},... | collective-permute-start | bytes 491528 | tf_op jit(solution)/shard_map/ppermute | solution.py:60
  17.5 85.7 %all-gather.7.cloned.1.call-start = ((), (), s32[]{:S(2)}) async-start(), calls=%async_computation.1 | async-start | bytes 1638400 | tf_op jit(solution)/shard_map/all_gather | solution.py:88
  77.8 20.0 %collective-permute-start.1 = (bf16[4,3,64,512]{3,2,1,0:T(8,128)(2,1)S(1)}, bf16[4,3,64,512]{3,2,1,0:T(8,128)(2,1)S(1)}, u32[]{:S(2)}, u32[]{:S(2)}) collective-permute-start(bf16[4,3,64,512]{3,2,1,0:T(8,128)(2,1)S(1)} %slice.287.refs_1_), channel_id=1, source_target_pairs={{0,2},{2,0},{4,6},{6,4},{8,10},{10,8},{12,14},{14,12},{16,18},{18,... | collective-permute-start | bytes 2359304 | tf_op jit(solution)/shard_map/ppermute | solution.py:60
  81.9 18.2 %collective-permute-start.3 = (bf16[4,2,64,512]{3,2,1,0:T(8,128)(2,1)S(1)}, bf16[4,2,64,512]{3,2,1,0:T(8,128)(2,1)}, u32[]{:S(2)}, u32[]{:S(2)}) collective-permute-start(bf16[4,2,64,512]{3,2,1,0:T(8,128)(2,1)S(1)} %slice.288.refs_5_), channel_id=1, source_target_pairs={{0,4},{2,6},{4,0},{6,2},{8,12},{10,14},{12,8},{14,10},{16,20},{18,... | collective-permute-start | bytes 1572872 | tf_op jit(solution)/shard_map/ppermute | solution.py:60
  84.5 29.1 %collective-permute-start = (bf16[4,3,64,512]{3,2,1,0:T(8,128)(2,1)S(1)}, bf16[4,3,64,512]{3,2,1,0:T(8,128)(2,1)S(1)}, u32[]{:S(2)}, u32[]{:S(2)}) collective-permute-start(bf16[4,3,64,512]{3,2,1,0:T(8,128)(2,1)S(1)} %slice.287.refs_1_), channel_id=1, source_target_pairs={{0,4},{2,6},{4,0},{6,2},{8,12},{10,14},{12,8},{14,10},{16,20},{18,... | collective-permute-start | bytes 2359304 | tf_op jit(solution)/shard_map/ppermute | solution.py:60
  97.8 32.1 %collective-permute-start.2 = (bf16[4,3,64,512]{3,2,1,0:T(8,128)(2,1)S(1)}, bf16[4,3,64,512]{3,2,1,0:T(8,128)(2,1)}, u32[]{:S(2)}, u32[]{:S(2)}) collective-permute-start(bf16[4,3,64,512]{3,2,1,0:T(8,128)(2,1)S(1)} %collective-permute-done.1.refs_3_), channel_id=1, source_target_pairs={{0,4},{2,6},{4,0},{6,2},{8,12},{10,14},{12,8},{14,10},{16,20},{18,... | collective-permute-start | bytes 2359304 | tf_op jit(solution)/shard_map/ppermute | solution.py:60
  100.1 24.7 %collective-permute-start.5 = (bf16[4,2,64,512]{3,2,1,0:T(8,128)(2,1)}, bf16[4,2,64,512]{3,2,1,0:T(8,128)(2,1)}, u32[]{:S(2)}, u32[]{:S(2)}) collective-permute-start(bf16[4,2,64,512]{3,2,1,0:T(8,128)(2,1)} %collective-permute-done.3.refs_6_), channel_id=1, source_target_pairs={{0,2},{2,0},{4,6},{6,4},{8,10},{10,8},{12,14},{14,12},{16,18},{18,... | collective-permute-start | bytes 1572872 | tf_op jit(solution)/shard_map/ppermute | solution.py:60
  105.3 52.2 %collective-permute-start.18 = (bf16[4,3,64,512]{3,2,1,0:T(8,128)(2,1)}, bf16[4,3,64,512]{3,2,1,0:T(8,128)(2,1)}, u32[]{:S(2)}, u32[]{:S(2)}) collective-permute-start(bf16[4,3,64,512]{3,2,1,0:T(8,128)(2,1)} %slice.303.refs_2_), channel_id=1, source_target_pairs={{0,2},{2,0},{4,6},{6,4},{8,10},{10,8},{12,14},{14,12},{16,18},{18,... | collective-permute-start | bytes 2359304 | tf_op jit(solution)/shard_map/ppermute | solution.py:60
  153.5 50.3 %collective-permute-start.16 = (bf16[16,96,512]{2,1,0:T(8,128)(2,1)}, bf16[16,96,512]{2,1,0:T(8,128)(2,1)}, u32[]{:S(2)}, u32[]{:S(2)}) collective-permute-start(bf16[16,96,512]{2,1,0:T(8,128)(2,1)} %get-tuple-element.38.refs_0_), channel_id=1, source_target_pairs={{0,1},{1,0},{2,3},{3,2},{4,5},{5,4},{6,7},{7,6},{8,9},{9,8},{10,11... | collective-permute-start | bytes 4718600 | tf_op jit(solution)/shard_map/ppermute | solution.py:65
  157.0 30.4 %collective-permute-start.17 = (bf16[4,3,64,512]{3,2,1,0:T(8,128)(2,1)}, bf16[4,3,64,512]{3,2,1,0:T(8,128)(2,1)}, u32[]{:S(2)}, u32[]{:S(2)}) collective-permute-start(bf16[4,3,64,512]{3,2,1,0:T(8,128)(2,1)} %slice.303.refs_2_), channel_id=1, source_target_pairs={{0,4},{2,6},{4,0},{6,2},{8,12},{10,14},{12,8},{14,10},{16,20},{18,... | collective-permute-start | bytes 2359304 | tf_op jit(solution)/shard_map/ppermute | solution.py:60
  157.5 46.3 %collective-permute-start.19 = (bf16[4,3,64,512]{3,2,1,0:T(8,128)(2,1)}, bf16[4,3,64,512]{3,2,1,0:T(8,128)(2,1)}, u32[]{:S(2)}, u32[]{:S(2)}) collective-permute-start(bf16[4,3,64,512]{3,2,1,0:T(8,128)(2,1)} %collective-permute-done.18.refs_4_), channel_id=1, source_target_pairs={{0,4},{2,6},{4,0},{6,2},{8,12},{10,14},{12,8},{14,10},{16,20},{18,... | collective-permute-start | bytes 2359304 | tf_op jit(solution)/shard_map/ppermute | solution.py:60
  159.0 15.2 %collective-permute-start.21 = (bf16[4,2,64,512]{3,2,1,0:T(8,128)(2,1)}, bf16[4,2,64,512]{3,2,1,0:T(8,128)(2,1)}, u32[]{:S(2)}, u32[]{:S(2)}) collective-permute-start(bf16[4,2,64,512]{3,2,1,0:T(8,128)(2,1)} %slice.304.refs_6_), channel_id=1, source_target_pairs={{0,2},{2,0},{4,6},{6,4},{8,10},{10,8},{12,14},{14,12},{16,18},{18,... | collective-permute-start | bytes 1572872 | tf_op jit(solution)/shard_map/ppermute | solution.py:60
  170.5 16.9 %collective-permute-start.22 = (bf16[4,2,64,512]{3,2,1,0:T(8,128)(2,1)}, bf16[4,2,64,512]{3,2,1,0:T(8,128)(2,1)}, u32[]{:S(2)}, u32[]{:S(2)}) collective-permute-start(bf16[4,2,64,512]{3,2,1,0:T(8,128)(2,1)} %collective-permute-done.20.refs_7_), channel_id=1, source_target_pairs={{0,2},{2,0},{4,6},{6,4},{8,10},{10,8},{12,14},{14,12},{16,18},{18,... | collective-permute-start | bytes 1572872 | tf_op jit(solution)/shard_map/ppermute | solution.py:60
  224.4 72.5 %collective-permute-start.25 = (bf16[5,512,512]{2,1,0:T(8,128)(2,1)}, bf16[5,512,512]{2,1,0:T(8,128)(2,1)}, u32[]{:S(2)}, u32[]{:S(2)}) collective-permute-start(bf16[5,512,512]{2,1,0:T(8,128)(2,1)} %get-tuple-element.43), channel_id=1, source_target_pairs={{0,1},{1,0},{2,3},{3,2},{4,5},{5,4},{6,7},{7,6},{8,9},{9,8},{10,11... | collective-permute-start | bytes 7864328 | tf_op jit(solution)/shard_map/ppermute | solution.py:65
  235.1 25.6 %collective-permute-start.39 = (bf16[2,4,128,512]{3,2,1,0:T(8,128)(2,1)S(1)}, bf16[2,4,128,512]{3,2,1,0:T(8,128)(2,1)S(1)}, u32[]{:S(2)}, u32[]{:S(2)}) collective-permute-start(bf16[2,4,128,512]{3,2,1,0:T(8,128)(2,1)S(1)} %bitcast.128), channel_id=1, source_target_pairs={{0,2},{2,0},{4,6},{6,4},{8,10},{10,8},{12,14},{14,12},{16,18},{18,... | collective-permute-start | bytes 3145736 | tf_op jit(solution)/shard_map/ppermute | solution.py:60
  246.5 37.6 %collective-permute-start.37 = (bf16[2,4,192,512]{3,2,1,0:T(8,128)(2,1)}, bf16[2,4,192,512]{3,2,1,0:T(8,128)(2,1)}, u32[]{:S(2)}, u32[]{:S(2)}) collective-permute-start(bf16[2,4,192,512]{3,2,1,0:T(8,128)(2,1)} %bitcast.42), channel_id=1, source_target_pairs={{0,4},{2,6},{4,0},{6,2},{8,12},{10,14},{12,8},{14,10},{16,20},{18,... | collective-permute-start | bytes 4718600 | tf_op jit(solution)/shard_map/ppermute | solution.py:60
  247.0 49.9 %collective-permute-start.24 = (bf16[16,96,512]{2,1,0:T(8,128)(2,1)}, bf16[16,96,512]{2,1,0:T(8,128)(2,1)}, u32[]{:S(2)}, u32[]{:S(2)}) collective-permute-start(bf16[16,96,512]{2,1,0:T(8,128)(2,1)} %get-tuple-element.41.refs_0_.grads), channel_id=1, source_target_pairs={{0,1},{1,0},{2,3},{3,2},{4,5},{5,4},{6,7},{7,6},{8,9},{9,8},{10,11... | collective-permute-start | bytes 4718600 | tf_op jit(solution)/shard_map/ppermute | solution.py:65
  262.6 32.0 %collective-permute-start.40 = (bf16[4,128,512]{2,1,0:T(8,128)(2,1)S(1)}, bf16[4,128,512]{2,1,0:T(8,128)(2,1)}, u32[]{:S(2)}, u32[]{:S(2)}) collective-permute-start(bf16[4,128,512]{2,1,0:T(8,128)(2,1)S(1)} %fusion.21), channel_id=1, source_target_pairs={{0,4},{2,6},{4,0},{6,2},{8,12},{10,14},{12,8},{14,10},{16,20},{18,... | collective-permute-start | bytes 1572872 | tf_op jit(solution)/shard_map/ppermute | solution.py:60
  270.0 152.5 %collective-permute-start.27 = (bf16[5,512,512]{2,1,0:T(8,128)(2,1)}, bf16[5,512,512]{2,1,0:T(8,128)(2,1)}, u32[]{:S(2)}, u32[]{:S(2)}) collective-permute-start(bf16[5,512,512]{2,1,0:T(8,128)(2,1)} %get-tuple-element.48), channel_id=1, source_target_pairs={{0,1},{1,0},{2,3},{3,2},{4,5},{5,4},{6,7},{7,6},{8,9},{9,8},{10,11... | collective-permute-start | bytes 7864328 | tf_op jit(solution)/shard_map/ppermute | solution.py:65
  284.0 91.6 %collective-permute-start.23 = (bf16[16,96,512]{2,1,0:T(8,128)(2,1)}, bf16[16,96,512]{2,1,0:T(8,128)(2,1)}, u32[]{:S(2)}, u32[]{:S(2)}) collective-permute-start(bf16[16,96,512]{2,1,0:T(8,128)(2,1)} %get-tuple-element.40.refs_0_), channel_id=1, source_target_pairs={{0,1},{1,0},{2,3},{3,2},{4,5},{5,4},{6,7},{7,6},{8,9},{9,8},{10,11... | collective-permute-start | bytes 4718600 | tf_op jit(solution)/shard_map/ppermute | solution.py:65
  316.8 20.3 %collective-permute-start.38 = (bf16[4,192,512]{2,1,0:T(8,128)(2,1)}, bf16[4,192,512]{2,1,0:T(8,128)(2,1)}, u32[]{:S(2)}, u32[]{:S(2)}) collective-permute-start(bf16[4,192,512]{2,1,0:T(8,128)(2,1)} %fusion.18), channel_id=1, source_target_pairs={{0,2},{2,0},{4,6},{6,4},{8,10},{10,8},{12,14},{14,12},{16,18},{18,... | collective-permute-start | bytes 2359304 | tf_op jit(solution)/shard_map/ppermute | solution.py:60
  321.5 17.7 %collective-permute-start.44 = (f32[28,1280]{1,0:T(8,128)S(1)}, f32[28,1280]{1,0:T(8,128)S(1)}, u32[]{:S(2)}, u32[]{:S(2)}) collective-permute-start(f32[28,1280]{1,0:T(8,128)S(1)} %fusion.22), channel_id=1, source_target_pairs={{0,1},{1,0},{2,3},{3,2},{4,5},{5,4},{6,7},{7,6},{8,9},{9,8},{10,11... | collective-permute-start | bytes 430088 | tf_op jit(solution)/shard_map/ppermute | solution.py:65
  340.0 35.6 %collective-permute-start.42 = (bf16[320,512]{1,0:T(8,128)(2,1)S(1)}, bf16[320,512]{1,0:T(8,128)(2,1)S(1)}, u32[]{:S(2)}, u32[]{:S(2)}) collective-permute-start(bf16[320,512]{1,0:T(8,128)(2,1)S(1)} %pad_maximum_fusion.6), channel_id=1, source_target_pairs={{0,16},{2,18},{4,20},{6,22},{8,24},{10,26},{12,28},{14,30},{16,0},... | collective-permute-start | bytes 983048 | tf_op jit(solution)/shard_map/ppermute | solution.py:60
  360.9 57.5 %collective-permute-start.30 = (bf16[2,4,272,512]{3,2,1,0:T(8,128)(2,1)S(1)}, bf16[2,4,272,512]{3,2,1,0:T(8,128)(2,1)}, u32[]{:S(2)}, u32[]{:S(2)}) collective-permute-start(bf16[2,4,272,512]{3,2,1,0:T(8,128)(2,1)S(1)} %bitcast.127), channel_id=1, source_target_pairs={{0,4},{2,6},{4,0},{6,2},{8,12},{10,14},{12,8},{14,10},{16,20},{18,... | collective-permute-start | bytes 6684680 | tf_op jit(solution)/shard_map/ppermute | solution.py:60
  377.6 36.0 %collective-permute-start.32 = (bf16[2,4,208,512]{3,2,1,0:T(8,128)(2,1)}, bf16[2,4,208,512]{3,2,1,0:T(8,128)(2,1)}, u32[]{:S(2)}, u32[]{:S(2)}) collective-permute-start(bf16[2,4,208,512]{3,2,1,0:T(8,128)(2,1)} %bitcast.30), channel_id=1, source_target_pairs={{0,2},{2,0},{4,6},{6,4},{8,10},{10,8},{12,14},{14,12},{16,18},{18,... | collective-permute-start | bytes 5111816 | tf_op jit(solution)/shard_map/ppermute | solution.py:60
  389.4 33.2 %collective-permute-start.26 = (bf16[16,96,512]{2,1,0:T(8,128)(2,1)}, bf16[16,96,512]{2,1,0:T(8,128)(2,1)}, u32[]{:S(2)}, u32[]{:S(2)}) collective-permute-start(bf16[16,96,512]{2,1,0:T(8,128)(2,1)} %get-tuple-element.46.refs_0_.grads), channel_id=1, source_target_pairs={{0,1},{1,0},{2,3},{3,2},{4,5},{5,4},{6,7},{7,6},{8,9},{9,8},{10,11... | collective-permute-start | bytes 4718600 | tf_op jit(solution)/shard_map/ppermute | solution.py:65
  416.9 19.9 %collective-permute-start.33 = (bf16[4,208,512]{2,1,0:T(8,128)(2,1)}, bf16[4,208,512]{2,1,0:T(8,128)(2,1)}, u32[]{:S(2)}, u32[]{:S(2)}) collective-permute-start(bf16[4,208,512]{2,1,0:T(8,128)(2,1)} %fusion.15), channel_id=1, source_target_pairs={{0,4},{2,6},{4,0},{6,2},{8,12},{10,14},{12,8},{14,10},{16,20},{18,... | collective-permute-start | bytes 2555912 | tf_op jit(solution)/shard_map/ppermute | solution.py:60
  422.1 22.2 %collective-permute-start.31 = (bf16[4,272,512]{2,1,0:T(8,128)(2,1)}, bf16[4,272,512]{2,1,0:T(8,128)(2,1)}, u32[]{:S(2)}, u32[]{:S(2)}) collective-permute-start(bf16[4,272,512]{2,1,0:T(8,128)(2,1)} %fusion.9), channel_id=1, source_target_pairs={{0,2},{2,0},{4,6},{6,4},{8,10},{10,8},{12,14},{14,12},{16,18},{18,... | collective-permute-start | bytes 3342344 | tf_op jit(solution)/shard_map/ppermute | solution.py:60
  447.0 28.2 %collective-permute-start.35 = (bf16[480,512]{1,0:T(8,128)(2,1)S(1)}, bf16[480,512]{1,0:T(8,128)(2,1)S(1)}, u32[]{:S(2)}, u32[]{:S(2)}) collective-permute-start(bf16[480,512]{1,0:T(8,128)(2,1)S(1)} %pad_maximum_fusion.2), channel_id=1, source_target_pairs={{0,16},{2,18},{4,20},{6,22},{8,24},{10,26},{12,28},{14,30},{16,0},... | collective-permute-start | bytes 1474568 | tf_op jit(solution)/shard_map/ppermute | solution.py:60
  449.5 37.1 %collective-permute-start.36 = (bf16[480,512]{1,0:T(8,128)(2,1)S(1)}, bf16[480,512]{1,0:T(8,128)(2,1)S(1)}, u32[]{:S(2)}, u32[]{:S(2)}) collective-permute-start(bf16[480,512]{1,0:T(8,128)(2,1)S(1)} %pad_maximum_fusion.3), channel_id=1, source_target_pairs={{0,24},{2,26},{4,28},{6,30},{8,0},{10,2},{12,4},{14,6},{16,8},{18,... | collective-permute-start | bytes 1474568 | tf_op jit(solution)/shard_map/ppermute | solution.py:60
  449.6 37.0 %collective-permute-start.34 = (bf16[480,512]{1,0:T(8,128)(2,1)S(1)}, bf16[480,512]{1,0:T(8,128)(2,1)S(1)}, u32[]{:S(2)}, u32[]{:S(2)}) collective-permute-start(bf16[480,512]{1,0:T(8,128)(2,1)S(1)} %pad_maximum_fusion.1), channel_id=1, source_target_pairs={{0,8},{2,10},{4,12},{6,14},{8,16},{10,18},{12,20},{14,22},{16,24},... | collective-permute-start | bytes 1474568 | tf_op jit(solution)/shard_map/ppermute | solution.py:60
  (61 other events, 674.9 us)
Sparse Core Ops, SparseCore 0:
  17.6 33.8 all-gather.4
  67.9 33.5 all-gather.6
